TPU v7x, 1024 devices: a whole 4x4x32 slice. The times are simulated.
1024 devices in a mesh: clip: 16 (over y, x), tm: 64 (over z, core).
Axes of the slice: x: 4, y: 4, z: 32, core: 2. Of those that a mesh axis runs over, the one named last changes fastest.
Arguments:
- embeddings: bfloat16 [256, 256, 768], P('clip', 'tm'), may hold values from -6 to 6
- lengths: int32 [256], replicated, may hold values from 64 to 256, as said below
- pairs: int32 [2048, 2], replicated, may hold values from 0 to 255, as said below
- scaled_weight: float32 [2048], P(('clip', 'tm')), may hold values from 64 to 1024
Outputs:
- pair_loss: float32 [2048], P(('clip', 'tm'))
- grad_embeddings: bfloat16 [256, 256, 768], P('clip', 'tm')
Inputs may be any that keep to these rules, and one draw needn't show every extreme that they name: `lengths`: each clip's length in frames; some clip has exactly 256. `pairs`: clip ids. The first clip of row r lies in owner shard r // 128, i.e. among ids of that shard's 16 clips; the partner differs from the first clip. The rows of one owner shard name at most 4 distinct partner clips of any one shard, and exactly 4 of some shard.
All inputs are finite; a program needn't handle non-finite values.
Results may differ from a plain program's by a relative error of at most 0.025.
Values may be sent and summed in bfloat16 or wider, within the bound.
No kernel may reach another device: no remote copies, remote signals or barrier semaphores. Data moves between devices by JAX's collectives and lax.ppermute only.
A program may use at most 32 MiB of HBM per device.

v0:
```python
import math

import jax
import jax.numpy as jnp
from jax import lax
from jax.sharding import PartitionSpec as P

score_scale = 2.0
spread_floor = 1.0
log_weight = 0.1
epsilon = 1e-06


def normalize(values):
    as_float = values.astype(jnp.float32)
    scaled = as_float * lax.rsqrt(jnp.mean(as_float * as_float, axis=-1, keepdims=True) + epsilon)
    return scaled.astype(jnp.bfloat16)


def cross_scores(left, right, factor):
    products = lax.dot_general(
        left, right, (((1,), (1,)), ((), ())), preferred_element_type=jnp.float32
    )
    return products * factor


def pair_value(first_clip, partner_clip, len_first, len_partner):
    frames = first_clip.shape[0]
    feature = first_clip.shape[1]
    factor = score_scale / math.sqrt(feature)
    n_first = normalize(first_clip)
    n_partner = normalize(partner_clip)
    positions = jnp.arange(frames, dtype=jnp.int32)
    forward_scores = cross_scores(n_first, n_partner, factor)
    forward_exp = jnp.where((positions < len_partner)[None, :], jnp.exp(forward_scores), 0.0)
    forward_prob = (forward_exp / jnp.sum(forward_exp, axis=1, keepdims=True)).astype(jnp.bfloat16)
    soft_match = jnp.dot(forward_prob, n_partner, preferred_element_type=jnp.float32).astype(
        jnp.bfloat16
    )
    backward_scores = cross_scores(soft_match, n_first, factor)
    backward_exp = jnp.where((positions < len_first)[None, :], jnp.exp(backward_scores), 0.0)
    back_prob = backward_exp / jnp.sum(backward_exp, axis=1, keepdims=True)
    frame_time = positions.astype(jnp.float32)
    mean_time = jnp.sum(back_prob * frame_time[None, :], axis=1)
    offsets = frame_time[None, :] - mean_time[:, None]
    spread = jnp.sum(back_prob * offsets * offsets, axis=1) + spread_floor
    missed = frame_time - mean_time
    frame_terms = missed * missed / spread + log_weight * jnp.log(spread)
    valid_rows = positions < len_first
    return jnp.sum(jnp.where(valid_rows, frame_terms, 0.0)) / len_first.astype(jnp.float32)


def pair_grads(first_clip, partner_clip, len_first, len_partner, weight):
    value, pullback = jax.vjp(
        lambda left, right: pair_value(left, right, len_first, len_partner),
        first_clip,
        partner_clip,
    )
    grad_first, grad_partner = pullback(weight)
    return (value, grad_first, grad_partner)


def shards(embeddings, lengths, pairs, scaled_weight):
    clip_devices = lax.axis_size("clip")
    time_devices = lax.axis_size("tm")
    clip_count, frame_block, feature = embeddings.shape
    owner_index = lax.axis_index("clip")
    time_index = lax.axis_index("tm")
    per_device = scaled_weight.shape[0]
    per_owner = per_device * time_devices
    row_width = frame_block * feature
    grouped = pairs.reshape(clip_devices, per_owner, 2)
    owned_pairs = lax.dynamic_index_in_dim(grouped, owner_index, 0, keepdims=False)
    first_slot = owned_pairs[:, 0] - owner_index * clip_count
    flattened = embeddings.reshape(clip_count, row_width)
    first_rows = jnp.take(flattened, first_slot, axis=0)
    everything = lax.all_gather(flattened, "clip", axis=0, tiled=True)
    partner_rows = jnp.take(everything, owned_pairs[:, 1], axis=0)
    outgoing_pairs = jnp.stack([first_rows, partner_rows], axis=1).reshape(
        time_devices, per_device, 2, frame_block, feature
    )
    gathered_frames = lax.all_to_all(outgoing_pairs, "tm", split_axis=0, concat_axis=3, tiled=True)[
        0
    ]
    my_ids = lax.dynamic_slice_in_dim(owned_pairs, time_index * per_device, per_device, 0)
    len_first = jnp.take(lengths, my_ids[:, 0])
    len_partner = jnp.take(lengths, my_ids[:, 1])
    losses, grad_first, grad_partner = jax.vmap(pair_grads)(
        gathered_frames[:, 0], gathered_frames[:, 1], len_first, len_partner, scaled_weight
    )
    grad_pairs = jnp.stack([grad_first, grad_partner], axis=1)[None]
    returned = lax.all_to_all(grad_pairs, "tm", split_axis=3, concat_axis=0, tiled=True)
    returned = returned.reshape(per_owner, 2, row_width)
    first_hot = (jnp.arange(clip_count, dtype=jnp.int32)[:, None] == first_slot[None, :]).astype(
        jnp.bfloat16
    )
    first_sum = jnp.dot(first_hot, returned[:, 0], preferred_element_type=jnp.float32)
    clip_hot = (
        jnp.arange(clip_devices * clip_count, dtype=jnp.int32)[:, None]
        == owned_pairs[:, 1][None, :]
    ).astype(jnp.bfloat16)
    partner_sum = jnp.dot(clip_hot, returned[:, 1], preferred_element_type=jnp.float32)
    partner_total = lax.psum_scatter(
        partner_sum.astype(jnp.bfloat16), "clip", scatter_dimension=0, tiled=True
    ).astype(jnp.float32)
    gradient = (
        (first_sum + partner_total).astype(jnp.bfloat16).reshape(clip_count, frame_block, feature)
    )
    return (losses, gradient)


def solution(mesh):
    in_specs = (P("clip", "tm", None), P(), P(), P(("clip", "tm")))
    out_specs = (P(("clip", "tm")), P("clip", "tm", None))
    return jax.shard_map(shards, mesh=mesh, in_specs=in_specs, out_specs=out_specs, check_vma=False)
```

profile of v0, /device:TPU:24, one launch (start us, length us, event | category | flops | bytes accessed | tf_op | source)
XLA Modules:
  0.0 557.1 jit_solution(7754754837923135342)
XLA Ops:
  7.2 1.5 copy.37
  8.8 0.8 copy.41
  9.9 1.0 gather_fusion
  11.6 87.8 %all-gather.2.cloned.1.call-done = bf16[256,3072]{1,0:T(8,128)(2,1)} async-done(((bf16[16,3072]{1,0:T(8,128)(2,1)}), bf16[256,3072]{1,0:T(8,128)(2,1)}) %all-gather.2.cloned.1.call-update) | async-done | bytes 1572880 | tf_op jit(solution)/shard_map/all_gather | solution.py:77
  99.4 3.4 gather_fusion.1
  103.4 1.0 bitcast_select_fusion
  104.4 2.2 pad_maximum_fusion
  106.6 23.7 %all-to-all-start = ((bf16[64,2,2,4,768]{4,3,1,2,0:T(4,128)(2,1)}), bf16[64,2,2,4,768]{4,3,1,2,0:T(4,128)(2,1)S(1)}, u32[]{:S(2)}, u32[]{:S(2)}) async-start(bf16[64,2,2,4,768]{4,3,1,2,0:T(4,128)(2,1)} %pad_maximum_fusion), calls=%async_computation | async-start | bytes 3145728 | tf_op jit(solution)/shard_map/all_to_all | solution.py:82
  130.9 0.6 gather_fusion.3
  131.5 0.6 gather_fusion.2
  132.3 153.5 %all-to-all-done = bf16[64,2,2,4,768]{4,3,1,2,0:T(4,128)(2,1)S(1)} async-done(((bf16[64,2,2,4,768]{4,3,1,2,0:T(4,128)(2,1)}), bf16[64,2,2,4,768]{4,3,1,2,0:T(4,128)(2,1)S(1)}, u32[]{:S(2)}, u32[]{:S(2)}) %all-to-all-start) | async-done | bytes 1572896 | tf_op jit(solution)/shard_map/all_to_all | solution.py:82
  287.3 0.9 select_reduce_fusion.1
  290.4 0.7 convolution_convert_fusion.3
  292.0 0.6 convolution_convert_fusion.2
  293.0 0.9 fusion.5
  293.9 0.7 fusion.15
  294.8 1.6 copy.30
  296.5 156.7 %all_to_all.30 = bf16[1,2,2,256,768]{4,1,2,0,3:T(2,128)(2,1)S(1)} all-to-all(bf16[1,2,2,256,768]{4,1,2,0,3:T(2,128)(2,1)S(1)} %copy.30), channel_id=1, replica_groups=mesh['clip'=16,'tm'=64] {'tm'}, dimensions={3} | all-to-all | bytes 3145728 | tf_op jit(solution)/shard_map/all_to_all | solution.py:92
  453.2 0.6 copy.40
  453.8 1.2 reshape.187
  455.0 1.7 convolution_convert_fusion
  457.2 91.2 %reduce-scatter.2.cloned.1.call-done = bf16[16,3072]{1,0:T(8,128)(2,1)} async-done(((bf16[256,3072]{1,0:T(8,128)(2,1)}), bf16[16,3072]{1,0:T(8,128)(2,1)}) %reduce-scatter.2.cloned.1.call-update) | async-done | bytes 98320 | tf_op jit(solution)/shard_map/reduce_scatter | solution.py:103
  548.5 1.1 fusion
  549.6 0.7 reshape.188
  (54 shorter events, 7.9 us)
Async XLA Ops:
  7.2 123.7 %copy-start = (s32[256]{0:T(256)S(1)}, s32[256]{0:T(256)}, u32[]{:S(2)}) copy-start(s32[256]{0:T(256)} %param.7) | copy-start | bytes 3076
  7.2 92.2 %all-gather.2.cloned.1.call-start = ((), (), s32[]{:S(2)}) async-start(), calls=%async_computation.3 | async-start | bytes 1671168 | tf_op jit(solution)/shard_map/all_gather | solution.py:77
  8.8 1.2 copy-start.1
  106.6 25.7 %copy-start.2 = (f32[2]{0:T(128)S(1)}, f32[2]{0:T(128)}, u32[]{:S(2)}) copy-start(f32[2]{0:T(128)} %param.9) | copy-start | bytes 28
  106.6 179.3 %all-to-all-start = ((bf16[64,2,2,4,768]{4,3,1,2,0:T(4,128)(2,1)}), bf16[64,2,2,4,768]{4,3,1,2,0:T(4,128)(2,1)S(1)}, u32[]{:S(2)}, u32[]{:S(2)}) async-start(bf16[64,2,2,4,768]{4,3,1,2,0:T(4,128)(2,1)} %pad_maximum_fusion), calls=%async_computation | async-start | bytes 3145728 | tf_op jit(solution)/shard_map/all_to_all | solution.py:82
  130.3 418.2 %reduce-scatter.2.cloned.1.call-start = ((), (), s32[]{:S(2)}) async-start(), calls=%async_computation.4 | async-start | bytes 1671168 | tf_op jit(solution)/shard_map/reduce_scatter | solution.py:103
Sparse Core Ops, SparseCore 0:
  12.8 86.5 all-gather.1
  456.8 91.5 reduce-scatter.1
where the time goes:
time: 558 us; the launch traced here: 557 us
  waiting for transfers between devices  333 us (60%)
  blocking collectives  157 us (28%)
  starting transfers between devices  23.9 us (4%)
  local copies, waits for them, and re-layouts  14.9 us (3%)
  between operations  14.3 us (3%)
  matrix products  8.23 us (1%)
  other arithmetic  6.36 us (1%)
    all_to_all x1, blocking collectives, shards(): lax.all_to_all(grad_pairs, 'tm', split_axis=3, concat_axis=0, tiled=True)  157 us
    all_to_all x1, waiting for transfers between devices, shards(): lax.all_to_all(outgoing_pairs, 'tm', split_axis=0, concat_axis=3, tiled=T...  154 us
    reduce_scatter x1, waiting for transfers between devices, shards(): lax.psum_scatter(partner_sum.astype(jnp.bfloat16), 'clip', scatter_dimens...  91.2 us
    all_gather x1, waiting for transfers between devices, shards(): everything = lax.all_gather(flattened, 'clip', axis=0, tiled=True)  87.8 us
    all_to_all x1, starting transfers between devices, shards(): lax.all_to_all(outgoing_pairs, 'tm', split_axis=0, concat_axis=3, tiled=T...  23.7 us
  transfers between devices with their start and end apart: 3, of which 3 were waited for; matrix products, arithmetic and copies ran while one was open for 1% of the time, Pallas kernels for 0%

commit v1 on v0

v1 whole, which is shorter than its diff:
```python
import math

import jax
import jax.numpy as jnp
from jax import lax
from jax.sharding import PartitionSpec as P

score_scale = 2.0
spread_floor = 1.0
log_weight = 0.1
epsilon = 1e-06
slots = 4


def dot(left, right, contract, out=jnp.float32):
    return lax.dot_general(left, right, (contract, ((), ())), preferred_element_type=out)


def split(values, parts):
    pieces = []
    for _ in range(parts):
        piece = lax.reduce_precision(values, 8, 7)
        pieces.append(piece.astype(jnp.bfloat16))
        values = values - piece
    return pieces


def with_scalars(rows, scalars):
    pieces = jnp.stack(split(scalars, 3))
    pad = ((0, 8 - pieces.shape[0]), (0, rows.shape[1] - pieces.shape[1]))
    return jnp.concatenate([rows, jnp.pad(pieces, pad)], axis=0)


def without_scalars(packed, count):
    pieces = packed[-8:-5, :count].astype(jnp.float32)
    return packed[:-8], (pieces[0] + pieces[1]) + pieces[2]


def pair_grads(n_first, n_partner, len_first, len_partner, weight):
    frames, feature = n_first.shape
    factor = score_scale / math.sqrt(feature)
    columns = lax.broadcasted_iota(jnp.int32, (frames, frames), 1)
    column_time = columns.astype(jnp.float32)
    scores = dot(n_first, n_partner, ((1,), (1,))) * factor
    forward_exp = jnp.where(columns < len_partner, jnp.exp(scores), 0.0)
    forward_prob = forward_exp / jnp.sum(forward_exp, axis=1, keepdims=True)
    prob = forward_prob.astype(jnp.bfloat16)
    high, low = split(scores, 2)
    backward_scores = dot(prob, high, ((1,), (1,))) + dot(prob, low, ((1,), (1,)))
    backward_exp = jnp.where(columns < len_first, jnp.exp(backward_scores), 0.0)
    back_prob = backward_exp / jnp.sum(backward_exp, axis=1, keepdims=True)
    mean_time = jnp.sum(back_prob * column_time, axis=1, keepdims=True)
    offsets = column_time - mean_time
    squares = offsets * offsets
    variance = jnp.sum(back_prob * squares, axis=1, keepdims=True)
    spread = variance + spread_floor
    rows = lax.broadcasted_iota(jnp.int32, (frames, 1), 0)
    missed = rows.astype(jnp.float32) - mean_time
    ratio = missed / spread
    terms = missed * ratio + log_weight * jnp.log(spread)
    valid = rows < len_first
    length = len_first.astype(jnp.float32)
    loss = jnp.sum(jnp.where(valid, terms, 0.0)) / length
    row_weight = jnp.where(valid, weight / length, 0.0)
    d_mean = -2.0 * ratio * row_weight
    d_spread = (log_weight / spread - ratio * ratio) * row_weight
    d_back = back_prob * (d_mean * offsets + d_spread * (squares - variance))
    d_back = d_back.astype(jnp.bfloat16)
    d_prob = dot(d_back, high, ((1,), (0,))) + dot(d_back, low, ((1,), (0,)))
    d_scores = forward_prob * (d_prob - jnp.sum(forward_prob * d_prob, axis=1, keepdims=True))
    d_scores = d_scores + dot(d_back, prob, ((0,), (0,)))
    d_scores = (d_scores * factor).astype(jnp.bfloat16)
    grad_first = dot(d_scores, n_partner, ((1,), (0,))).astype(jnp.bfloat16)
    grad_partner = dot(d_scores, n_first, ((0,), (0,))).astype(jnp.bfloat16)
    return loss, grad_first, grad_partner


def shards(embeddings, lengths, pairs, scaled_weight):
    owners = lax.axis_size("clip")
    times = lax.axis_size("tm")
    clip_count, block, feature = embeddings.shape
    per_device = scaled_weight.shape[0]
    per_owner = per_device * times
    row_width = block * feature
    spots = times // owners
    column = lax.axis_index("clip")
    time_index = lax.axis_index("tm")
    owner = time_index // spots
    spot = time_index % spots
    turn = (column - owner + owners) % owners
    place = turn * spots + spot

    long_range = [[a + spots * i for i in range(owners)] for a in range(spots)]
    home = [
        [((m + c) % owners) * times + spots * c + q for m in range(owners) for q in range(spots)]
        for c in range(owners)
    ]
    plane = [
        [((m + t // spots) % owners) * times + t for m in range(owners)] for t in range(times)
    ]
    swap = [
        (c * times + t, ((t // spots + c) % owners) * times + c * spots + t % spots)
        for c in range(owners)
        for t in range(times)
    ]
    back = [(there, here) for here, there in swap]
    both = ("clip", "tm")

    as_float = embeddings.astype(jnp.float32)
    scale = lax.rsqrt(jnp.mean(as_float * as_float, axis=-1, keepdims=True) + epsilon)
    normalized = (as_float * scale).astype(jnp.bfloat16)

    packed = with_scalars(normalized.reshape(clip_count * block, feature), scaled_weight)

    grouped = pairs.reshape(owners, per_owner, 2)
    clips = jnp.arange(owners * clip_count, dtype=jnp.int32)
    used = jnp.any(grouped[:, :, 1, None] == clips[None, None, :], axis=1)
    before = (clips[:, None] // clip_count == clips[None, :] // clip_count) & (
        clips[:, None] < clips[None, :]
    )
    rank = dot(used.astype(jnp.bfloat16), before.astype(jnp.bfloat16), ((1,), (0,)))
    rank = jnp.where(used, rank.astype(jnp.int32), -1)
    mine = lax.dynamic_slice_in_dim(rank, column * clip_count, clip_count, 1)
    slot_ids = jnp.arange(slots, dtype=jnp.int32)
    chosen = mine[:, None, :] == slot_ids[None, :, None]
    chosen = chosen.reshape(owners * slots, clip_count).astype(jnp.bfloat16)

    outgoing = dot(
        chosen, normalized.reshape(clip_count, row_width), ((1,), (0,)), jnp.bfloat16
    ).reshape(owners, slots * block, feature)
    outgoing = lax.all_to_all(
        outgoing, "tm", 0, 0, axis_index_groups=long_range, tiled=True
    )
    outgoing, packed = lax.optimization_barrier((outgoing, packed))
    firsts, weight = without_scalars(lax.ppermute(packed, both, swap), per_device)
    partners = lax.all_to_all(outgoing, both, 0, 0, axis_index_groups=plane, tiled=True)

    owned = lax.dynamic_index_in_dim(grouped, owner, 0, keepdims=False)
    owned_rank = lax.dynamic_index_in_dim(rank, owner, 0, keepdims=False)
    first_hot = (
        (owned[:, 0] - owner * clip_count)[:, None]
        == jnp.arange(clip_count, dtype=jnp.int32)[None, :]
    ).astype(jnp.bfloat16)
    partner_is = owned[:, 1][:, None] == clips[None, :]
    partner_slot = jnp.sum(jnp.where(partner_is, owned_rank[None, :], 0), axis=1)
    source = (owned[:, 1] // clip_count - owner + owners) % owners
    partner_slot = partner_slot + source * slots
    partner_hot = (
        partner_slot[:, None] == jnp.arange(owners * slots, dtype=jnp.int32)[None, :]
    ).astype(jnp.bfloat16)

    first_rows = dot(
        first_hot, firsts.reshape(clip_count, row_width), ((1,), (0,)), jnp.bfloat16
    ).reshape(times, per_device, block, feature)
    partner_rows = dot(
        partner_hot, partners.reshape(owners * slots, row_width), ((1,), (0,)), jnp.bfloat16
    ).reshape(times, per_device, block, feature)
    rows = jnp.concatenate([first_rows, partner_rows], axis=1)
    rows = rows.reshape(times, 2 * per_device * block, feature)
    frames = lax.all_to_all(rows, both, 0, 0, axis_index_groups=home, tiled=True)
    frames = frames.reshape(times, 2, per_device, block, feature).transpose(1, 2, 0, 3, 4)
    frames = frames.reshape(2, per_device, times * block, feature)

    my_ids = lax.dynamic_slice_in_dim(owned, place * per_device, per_device, 0)
    len_first = jnp.take(lengths, my_ids[:, 0])
    len_partner = jnp.take(lengths, my_ids[:, 1])
    losses, grad_first, grad_partner = jax.vmap(pair_grads)(
        frames[0], frames[1], len_first, len_partner, weight
    )

    grads = jnp.stack([grad_first, grad_partner]).reshape(
        2, per_device, times, block, feature
    )
    grads = grads.transpose(2, 0, 1, 3, 4).reshape(times, 2 * per_device * block, feature)
    returned = lax.all_to_all(grads, both, 0, 0, axis_index_groups=home, tiled=True)
    returned = returned.reshape(times, 2, per_device, row_width)
    first_back = returned[:, 0].reshape(per_owner, row_width)
    partner_back = returned[:, 1].reshape(per_owner, row_width)
    first_sum = dot(first_hot, first_back, ((0,), (0,))).astype(jnp.bfloat16)
    first_sum = with_scalars(first_sum.reshape(clip_count * block, feature), losses)
    first_sum = lax.ppermute(first_sum, both, back)
    partner_sum = dot(partner_hot, partner_back, ((0,), (0,))).astype(jnp.bfloat16)
    partner_sum = partner_sum.reshape(owners, slots * block, feature)
    partner_sum = lax.all_to_all(partner_sum, both, 0, 0, axis_index_groups=plane, tiled=True)
    partner_sum, first_sum = lax.optimization_barrier((partner_sum, first_sum))
    first_sum, losses = without_scalars(first_sum, per_device)
    partner_sum = lax.all_to_all(
        partner_sum, "tm", 0, 0, axis_index_groups=long_range, tiled=True
    )
    total = dot(chosen, partner_sum.reshape(owners * slots, row_width), ((0,), (0,)))
    total = total.reshape(clip_count, block, feature)
    total = total + first_sum.reshape(clip_count, block, feature).astype(jnp.float32)
    unit = as_float * scale
    gradient = scale * (total - unit * jnp.mean(total * unit, axis=-1, keepdims=True))
    return (losses, gradient.astype(jnp.bfloat16))


def solution(mesh):
    in_specs = (P("clip", "tm", None), P(), P(), P(("clip", "tm")))
    out_specs = (P(("clip", "tm")), P("clip", "tm", None))
    return jax.shard_map(shards, mesh=mesh, in_specs=in_specs, out_specs=out_specs, check_vma=False)
```

time: 558 us -> 301 us (0.54)
  waiting for transfers between devices: 333 us -> 149 us
  blocking collectives: 157 us -> 0 us
  starting transfers between devices: 23.9 us -> 117 us
  between operations: 14.3 us -> 1.16 us
    all_to_all x1 -> x0, blocking collectives: 157 us -> none  [shards(): lax.all_to_all(grad_pairs, 'tm', split_axis=3, concat_axis=0, tiled=True)]
    reduce_scatter x1 -> x0, waiting for transfers between devices: 91.2 us -> none  [shards(): lax.psum_scatter(partner_sum.astype(jnp.bfloat16), 'clip', scatter_dimens...]
    all_gather x1 -> x0, waiting for transfers between devices: 87.8 us -> none  [shards(): everything = lax.all_gather(flattened, 'clip', axis=0, tiled=True)]
    all_to_all x1 -> x6, starting transfers between devices: 23.7 us -> 99 us  [the longest x1 28.5 us: shards(): lax.all_to_all(outgoing, 'tm', 0, 0, axis_index_groups=long_range, tiled=...]
    ppermute x0 -> x2, starting transfers between devices: none -> 18 us  [the longest x1 9.64 us: shards(): first_sum = lax.ppermute(first_sum, both, back)]
    all_to_all x1 -> x6, waiting for transfers between devices: 154 us -> 137 us  [the longest x1 50.2 us: shards(): lax.all_to_all(partner_sum, 'tm', 0, 0, axis_index_groups=long_range, til...]
    ppermute x0 -> x2, waiting for transfers between devices: none -> 11.4 us  [the longest x1 11.4 us: shards(): first_sum = lax.ppermute(first_sum, both, back)]
    reshape x2 -> x13, local copies, waits for them, and re-layouts: 1.88 us -> 8.22 us  [the longest x1 2.02 us: shards(): rows = rows.reshape(times, 2 * per_device * block, feature)]
  transfers between devices with their start and end apart: 3 -> 8, of which waited for: 3 -> 6; matrix products, arithmetic and copies ran while one was open for 1% -> 2% of each run, Pallas kernels for 0% -> 0%
where the time goes in v1:
time: 301 us; the launch traced here: 300 us
  waiting for transfers between devices  149 us (50%)
  starting transfers between devices  117 us (39%)
  local copies, waits for them, and re-layouts  18 us (6%)
  matrix products  10.5 us (3%)
  other arithmetic  4.89 us (2%)
    all_to_all x1, waiting for transfers between devices, shards(): lax.all_to_all(partner_sum, 'tm', 0, 0, axis_index_groups=long_range, til...  50.2 us
    all_to_all x1, waiting for transfers between devices, shards(): lax.all_to_all(outgoing, 'tm', 0, 0, axis_index_groups=long_range, tiled=...  40.6 us
    all_to_all x1, starting transfers between devices, shards(): lax.all_to_all(outgoing, 'tm', 0, 0, axis_index_groups=long_range, tiled=...  28.5 us
    all_to_all x1, starting transfers between devices, shards(): lax.all_to_all(rows, both, 0, 0, axis_index_groups=home, tiled=True)  24 us
    all_to_all x1, waiting for transfers between devices, shards(): lax.all_to_all(grads, both, 0, 0, axis_index_groups=home, tiled=True)  21.6 us
    all_to_all x1, waiting for transfers between devices, shards(): lax.all_to_all(rows, both, 0, 0, axis_index_groups=home, tiled=True)  20 us
    all_to_all x1, starting transfers between devices, shards(): lax.all_to_all(partner_sum, 'tm', 0, 0, axis_index_groups=long_range, til...  19.9 us
    all_to_all x1, starting transfers between devices, shards(): lax.all_to_all(outgoing, both, 0, 0, axis_index_groups=plane, tiled=True)  12.9 us
  transfers between devices with their start and end apart: 8, of which 6 were waited for; matrix products, arithmetic and copies ran while one was open for 2% of the time, Pallas kernels for 0%

profile of v1, /device:TPU:24, one launch (start us, length us, event | category | flops | bytes accessed | tf_op | source)
XLA Modules:
  0.0 300.2 jit_solution(14833571688669993391)
XLA Ops:
  2.2 1.0 fusion.43
  4.4 1.0 reshape.479
  5.4 28.5 %all-to-all-start = ((bf16[16,16,768]{2,1,0:T(8,128)(2,1)}), bf16[16,16,768]{2,1,0:T(8,128)(2,1)}, u32[]{:S(2)}, u32[]{:S(2)}) async-start(bf16[16,16,768]{2,1,0:T(8,128)(2,1)} %reshape.479), calls=%async_computation | async-start | bytes 786432 | tf_op jit(solution)/shard_map/all_to_all | solution.py:131
  35.1 40.6 %all-to-all-done = bf16[16,16,768]{2,1,0:T(8,128)(2,1)} async-done(((bf16[16,16,768]{2,1,0:T(8,128)(2,1)}), bf16[16,16,768]{2,1,0:T(8,128)(2,1)}, u32[]{:S(2)}, u32[]{:S(2)}) %all-to-all-start) | async-done | bytes 393248 | tf_op jit(solution)/shard_map/all_to_all | solution.py:131
  75.6 8.4 %collective-permute-start = (bf16[72,768]{1,0:T(8,128)(2,1)S(1)}, bf16[72,768]{1,0:T(8,128)(2,1)S(1)}, u32[]{:S(2)}, u32[]{:S(2)}) collective-permute-start(bf16[72,768]{1,0:T(8,128)(2,1)S(1)} %pad_maximum_fusion.2), channel_id=1, source_target_pairs={{0,0},{1,1},{2,2},{3,3},{4,64},{5,65},{6,66},{7,67},{8,128},{9,129... | collective-permute-start | bytes 331784 | tf_op jit(solution)/shard_map/ppermute | solution.py:135
  84.0 12.9 %all-to-all-start.1 = ((bf16[16,16,768]{2,1,0:T(8,128)(2,1)}), bf16[16,16,768]{2,1,0:T(8,128)(2,1)S(1)}, u32[]{:S(2)}, u32[]{:S(2)}) async-start(bf16[16,16,768]{2,1,0:T(8,128)(2,1)} %all-to-all-done), calls=%async_computation.1 | async-start | bytes 786432 | tf_op jit(solution)/shard_map/all_to_all | solution.py:136
  99.1 5.0 %all-to-all-done.1 = bf16[16,16,768]{2,1,0:T(8,128)(2,1)S(1)} async-done(((bf16[16,16,768]{2,1,0:T(8,128)(2,1)}), bf16[16,16,768]{2,1,0:T(8,128)(2,1)S(1)}, u32[]{:S(2)}, u32[]{:S(2)}) %all-to-all-start.1) | async-done | bytes 393248 | tf_op jit(solution)/shard_map/all_to_all | solution.py:136
  104.9 2.0 copy.110
  106.9 24.0 %all-to-all-start.2 = ((bf16[64,16,768]{2,1,0:T(8,128)(2,1)}), bf16[64,16,768]{2,1,0:T(8,128)(2,1)S(1)}, u32[]{:S(2)}, u32[]{:S(2)}) async-start(bf16[64,16,768]{2,1,0:T(8,128)(2,1)} %copy.110), calls=%async_computation.2 | async-start | bytes 3145728 | tf_op jit(solution)/shard_map/all_to_all | solution.py:160
  132.7 20.0 %all-to-all-done.2 = bf16[64,16,768]{2,1,0:T(8,128)(2,1)S(1)} async-done(((bf16[64,16,768]{2,1,0:T(8,128)(2,1)}), bf16[64,16,768]{2,1,0:T(8,128)(2,1)S(1)}, u32[]{:S(2)}, u32[]{:S(2)}) %all-to-all-start.2) | async-done | bytes 1572896 | tf_op jit(solution)/shard_map/all_to_all | solution.py:160
  156.6 1.2 fusion.97
  157.8 1.2 convolution_add_fusion
  159.1 2.1 convolution_convert_fusion.3
  161.1 2.0 convolution_convert_fusion.2
  163.8 2.0 copy.123
  165.8 7.1 %all-to-all-start.3 = ((bf16[64,16,768]{2,1,0:T(8,128)(2,1)}), bf16[64,16,768]{2,1,0:T(8,128)(2,1)S(1)}, u32[]{:S(2)}, u32[]{:S(2)}) async-start(bf16[64,16,768]{2,1,0:T(8,128)(2,1)} %copy.123), calls=%async_computation.3 | async-start | bytes 3145728 | tf_op jit(solution)/shard_map/all_to_all | solution.py:175
  173.2 21.6 %all-to-all-done.3 = bf16[64,16,768]{2,1,0:T(8,128)(2,1)S(1)} async-done(((bf16[64,16,768]{2,1,0:T(8,128)(2,1)}), bf16[64,16,768]{2,1,0:T(8,128)(2,1)S(1)}, u32[]{:S(2)}, u32[]{:S(2)}) %all-to-all-start.3) | async-done | bytes 1572896 | tf_op jit(solution)/shard_map/all_to_all | solution.py:175
  195.3 2.0 fusion.114
  199.1 1.0 reshape.487
  200.1 6.5 %all-to-all-start.4 = ((bf16[16,16,768]{2,1,0:T(8,128)(2,1)}), bf16[16,16,768]{2,1,0:T(8,128)(2,1)}, u32[]{:S(2)}, u32[]{:S(2)}) async-start(bf16[16,16,768]{2,1,0:T(8,128)(2,1)} %reshape.487), calls=%async_computation.4 | async-start | bytes 786432 | tf_op jit(solution)/shard_map/all_to_all | solution.py:184
  207.0 9.6 %collective-permute-start.1 = (bf16[72,768]{1,0:T(8,128)(2,1)S(1)}, bf16[72,768]{1,0:T(8,128)(2,1)S(1)}, u32[]{:S(2)}, u32[]{:S(2)}) collective-permute-start(bf16[72,768]{1,0:T(8,128)(2,1)S(1)} %pad_maximum_fusion.3), channel_id=1, source_target_pairs={{0,0},{1,1},{2,2},{3,3},{64,4},{65,5},{66,6},{67,7},{128,8},{129,9... | collective-permute-start | bytes 331784 | tf_op jit(solution)/shard_map/ppermute | solution.py:181
  216.7 11.4 %collective-permute-done.1 = bf16[72,768]{1,0:T(8,128)(2,1)S(1)} collective-permute-done((bf16[72,768]{1,0:T(8,128)(2,1)S(1)}, bf16[72,768]{1,0:T(8,128)(2,1)S(1)}, u32[]{:S(2)}, u32[]{:S(2)}) %collective-permute-start.1) | collective-permute-done | bytes 110624 | tf_op jit(solution)/shard_map/ppermute | solution.py:181
  228.1 19.9 %all-to-all-start.5 = ((bf16[16,16,768]{2,1,0:T(8,128)(2,1)}), bf16[16,16,768]{2,1,0:T(8,128)(2,1)S(1)}, u32[]{:S(2)}, u32[]{:S(2)}) async-start(bf16[16,16,768]{2,1,0:T(8,128)(2,1)} %all-to-all-done.4), calls=%async_computation.5 | async-start | bytes 786432 | tf_op jit(solution)/shard_map/all_to_all | solution.py:187
  248.7 50.2 %all-to-all-done.5 = bf16[16,16,768]{2,1,0:T(8,128)(2,1)S(1)} async-done(((bf16[16,16,768]{2,1,0:T(8,128)(2,1)}), bf16[16,16,768]{2,1,0:T(8,128)(2,1)S(1)}, u32[]{:S(2)}, u32[]{:S(2)}) %all-to-all-start.5) | async-done | bytes 393248 | tf_op jit(solution)/shard_map/all_to_all | solution.py:187
  (92 shorter events, 17.9 us)
Async XLA Ops:
  0.6 130.7 %copy-start = (s32[256]{0:T(256)S(1)}, s32[256]{0:T(256)}, u32[]{:S(2)}) copy-start(s32[256]{0:T(256)} %param.7) | copy-start | bytes 3076
  0.6 33.3 %copy-start.2 = (bf16[16,4,768]{2,1,0:T(4,128)(2,1)S(1)}, bf16[16,4,768]{2,1,0:T(4,128)(2,1)}, u32[]{:S(2)}) copy-start(bf16[16,4,768]{2,1,0:T(4,128)(2,1)} %param.6) | copy-start | bytes 294916
  3.2 31.7 %copy-start.3 = (f32[2]{0:T(128)S(1)}, f32[2]{0:T(128)}, u32[]{:S(2)}) copy-start(f32[2]{0:T(128)} %param.9) | copy-start | bytes 28
  5.4 70.2 %all-to-all-start = ((bf16[16,16,768]{2,1,0:T(8,128)(2,1)}), bf16[16,16,768]{2,1,0:T(8,128)(2,1)}, u32[]{:S(2)}, u32[]{:S(2)}) async-start(bf16[16,16,768]{2,1,0:T(8,128)(2,1)} %reshape.479), calls=%async_computation | async-start | bytes 786432 | tf_op jit(solution)/shard_map/all_to_all | solution.py:131
  75.6 22.9 %collective-permute-start = (bf16[72,768]{1,0:T(8,128)(2,1)S(1)}, bf16[72,768]{1,0:T(8,128)(2,1)S(1)}, u32[]{:S(2)}, u32[]{:S(2)}) collective-permute-start(bf16[72,768]{1,0:T(8,128)(2,1)S(1)} %pad_maximum_fusion.2), channel_id=1, source_target_pairs={{0,0},{1,1},{2,2},{3,3},{4,64},{5,65},{6,66},{7,67},{8,128},{9,129... | collective-permute-start | bytes 331784 | tf_op jit(solution)/shard_map/ppermute | solution.py:135
  84.0 20.0 %all-to-all-start.1 = ((bf16[16,16,768]{2,1,0:T(8,128)(2,1)}), bf16[16,16,768]{2,1,0:T(8,128)(2,1)S(1)}, u32[]{:S(2)}, u32[]{:S(2)}) async-start(bf16[16,16,768]{2,1,0:T(8,128)(2,1)} %all-to-all-done), calls=%async_computation.1 | async-start | bytes 786432 | tf_op jit(solution)/shard_map/all_to_all | solution.py:136
  106.9 45.8 %all-to-all-start.2 = ((bf16[64,16,768]{2,1,0:T(8,128)(2,1)}), bf16[64,16,768]{2,1,0:T(8,128)(2,1)S(1)}, u32[]{:S(2)}, u32[]{:S(2)}) async-start(bf16[64,16,768]{2,1,0:T(8,128)(2,1)} %copy.110), calls=%async_computation.2 | async-start | bytes 3145728 | tf_op jit(solution)/shard_map/all_to_all | solution.py:160
  165.8 28.9 %all-to-all-start.3 = ((bf16[64,16,768]{2,1,0:T(8,128)(2,1)}), bf16[64,16,768]{2,1,0:T(8,128)(2,1)S(1)}, u32[]{:S(2)}, u32[]{:S(2)}) async-start(bf16[64,16,768]{2,1,0:T(8,128)(2,1)} %copy.123), calls=%async_computation.3 | async-start | bytes 3145728 | tf_op jit(solution)/shard_map/all_to_all | solution.py:175
  197.3 1.1 copy-start.1
  200.1 28.0 %all-to-all-start.4 = ((bf16[16,16,768]{2,1,0:T(8,128)(2,1)}), bf16[16,16,768]{2,1,0:T(8,128)(2,1)}, u32[]{:S(2)}, u32[]{:S(2)}) async-start(bf16[16,16,768]{2,1,0:T(8,128)(2,1)} %reshape.487), calls=%async_computation.4 | async-start | bytes 786432 | tf_op jit(solution)/shard_map/all_to_all | solution.py:184
  207.0 21.1 %collective-permute-start.1 = (bf16[72,768]{1,0:T(8,128)(2,1)S(1)}, bf16[72,768]{1,0:T(8,128)(2,1)S(1)}, u32[]{:S(2)}, u32[]{:S(2)}) collective-permute-start(bf16[72,768]{1,0:T(8,128)(2,1)S(1)} %pad_maximum_fusion.3), channel_id=1, source_target_pairs={{0,0},{1,1},{2,2},{3,3},{64,4},{65,5},{66,6},{67,7},{128,8},{129,9... | collective-permute-start | bytes 331784 | tf_op jit(solution)/shard_map/ppermute | solution.py:181
  228.1 70.7 %all-to-all-start.5 = ((bf16[16,16,768]{2,1,0:T(8,128)(2,1)}), bf16[16,16,768]{2,1,0:T(8,128)(2,1)S(1)}, u32[]{:S(2)}, u32[]{:S(2)}) async-start(bf16[16,16,768]{2,1,0:T(8,128)(2,1)} %all-to-all-done.4), calls=%async_computation.5 | async-start | bytes 786432 | tf_op jit(solution)/shard_map/all_to_all | solution.py:187

commit v2 on v1

--- a/solution.py
+++ b/solution.py
@@ -131,7 +131,6 @@
     outgoing = lax.all_to_all(
         outgoing, "tm", 0, 0, axis_index_groups=long_range, tiled=True
     )
-    outgoing, packed = lax.optimization_barrier((outgoing, packed))
     firsts, weight = without_scalars(lax.ppermute(packed, both, swap), per_device)
     partners = lax.all_to_all(outgoing, both, 0, 0, axis_index_groups=plane, tiled=True)
 
@@ -182,7 +181,6 @@
     partner_sum = dot(partner_hot, partner_back, ((0,), (0,))).astype(jnp.bfloat16)
     partner_sum = partner_sum.reshape(owners, slots * block, feature)
     partner_sum = lax.all_to_all(partner_sum, both, 0, 0, axis_index_groups=plane, tiled=True)
-    partner_sum, first_sum = lax.optimization_barrier((partner_sum, first_sum))
     first_sum, losses = without_scalars(first_sum, per_device)
     partner_sum = lax.all_to_all(
         partner_sum, "tm", 0, 0, axis_index_groups=long_range, tiled=True

time: 301 us -> 285 us (0.947); the launches traced: 300 us -> 280 us
  waiting for transfers between devices: 149 us -> 102 us
  blocking collectives: 0 us -> 41.7 us
  starting transfers between devices: 117 us -> 103 us
    all_to_all x1, waiting for transfers between devices: 50.2 us -> 0.01 us  [shards(): lax.all_to_all(partner_sum, 'tm', 0, 0, axis_index_groups=long_range, til...]
    all_to_all x0 -> x2, blocking collectives: none -> 41.7 us  [the longest x1 27.9 us: shards(): lax.all_to_all(grads, both, 0, 0, axis_index_groups=home, tiled=True)]
    ppermute x1, waiting for transfers between devices: 11.4 us -> 38.8 us  [shards(): first_sum = lax.ppermute(first_sum, both, back)]
    all_to_all x2 -> x0, waiting for transfers between devices: 21.6 us -> none  [the longest x1 21.6 us: shards(): lax.all_to_all(grads, both, 0, 0, axis_index_groups=home, tiled=True)]
    all_to_all x1, starting transfers between devices: 24 us -> 6.82 us  [shards(): lax.all_to_all(rows, both, 0, 0, axis_index_groups=home, tiled=True)]
    all_to_all x2 -> x0, starting transfers between devices: 13.6 us -> none  [the longest x1 7.1 us: shards(): lax.all_to_all(grads, both, 0, 0, axis_index_groups=home, tiled=True)]
    all_to_all x1, starting transfers between devices: 12.9 us -> 19.2 us  [shards(): lax.all_to_all(outgoing, both, 0, 0, axis_index_groups=plane, tiled=True)]
    ppermute x1, starting transfers between devices: 9.64 us -> 13.8 us  [shards(): first_sum = lax.ppermute(first_sum, both, back)]
  transfers between devices with their start and end apart: 8 -> 6, of which waited for: 6 -> 4; matrix products, arithmetic and copies ran while one was open for 2% -> 2% of each run, Pallas kernels for 0% -> 0%
where the time goes in v2:
time: 285 us; the launch traced here: 280 us
  starting transfers between devices  103 us (36%)
  waiting for transfers between devices  102 us (36%)
  blocking collectives  41.7 us (15%)
  local copies, waits for them, and re-layouts  15.9 us (6%)
  matrix products  11.3 us (4%)
  other arithmetic  4.9 us (2%)
    ppermute x1, waiting for transfers between devices, shards(): first_sum = lax.ppermute(first_sum, both, back)  38.8 us
    all_to_all x1, waiting for transfers between devices, shards(): lax.all_to_all(outgoing, 'tm', 0, 0, axis_index_groups=long_range, tiled=...  38 us
    all_to_all x1, starting transfers between devices, shards(): lax.all_to_all(outgoing, 'tm', 0, 0, axis_index_groups=long_range, tiled=...  28.5 us
    all_to_all x1, blocking collectives, shards(): lax.all_to_all(grads, both, 0, 0, axis_index_groups=home, tiled=True)  27.9 us
    all_to_all x1, starting transfers between devices, shards(): lax.all_to_all(partner_sum, 'tm', 0, 0, axis_index_groups=long_range, til...  22.5 us
    all_to_all x1, waiting for transfers between devices, shards(): lax.all_to_all(rows, both, 0, 0, axis_index_groups=home, tiled=True)  20 us
    all_to_all x1, starting transfers between devices, shards(): lax.all_to_all(outgoing, both, 0, 0, axis_index_groups=plane, tiled=True)  19.2 us
    all_to_all x1, blocking collectives, shards(): lax.all_to_all(partner_sum, both, 0, 0, axis_index_groups=plane, tiled=True)  13.9 us
  transfers between devices with their start and end apart: 6, of which 4 were waited for; matrix products, arithmetic and copies ran while one was open for 2% of the time, Pallas kernels for 0%

profile of v2, /device:TPU:24, one launch (start us, length us, event | category | flops | bytes accessed | tf_op | source)
XLA Modules:
  0.0 280.2 jit_solution(3633532304557450263)
XLA Ops:
  0.7 0.8 copy.175
  2.2 1.0 fusion.44
  3.2 1.0 fusion.135
  4.4 1.0 reshape.481
  5.4 28.5 %all-to-all-start = ((bf16[16,16,768]{2,1,0:T(8,128)(2,1)}), bf16[16,16,768]{2,1,0:T(8,128)(2,1)}, u32[]{:S(2)}, u32[]{:S(2)}) async-start(bf16[16,16,768]{2,1,0:T(8,128)(2,1)} %reshape.481), calls=%async_computation | async-start | bytes 786432 | tf_op jit(solution)/shard_map/all_to_all | solution.py:131
  34.2 12.5 %collective-permute-start = (bf16[72,768]{1,0:T(8,128)(2,1)S(1)}, bf16[72,768]{1,0:T(8,128)(2,1)S(1)}, u32[]{:S(2)}, u32[]{:S(2)}) collective-permute-start(bf16[72,768]{1,0:T(8,128)(2,1)S(1)} %pad_maximum_fusion.2), channel_id=1, source_target_pairs={{0,0},{1,1},{2,2},{3,3},{4,64},{5,65},{6,66},{7,67},{8,128},{9,129... | collective-permute-start | bytes 331784 | tf_op jit(solution)/shard_map/ppermute | solution.py:134
  47.6 38.0 %all-to-all-done = bf16[16,16,768]{2,1,0:T(8,128)(2,1)} async-done(((bf16[16,16,768]{2,1,0:T(8,128)(2,1)}), bf16[16,16,768]{2,1,0:T(8,128)(2,1)}, u32[]{:S(2)}, u32[]{:S(2)}) %all-to-all-start) | async-done | bytes 393248 | tf_op jit(solution)/shard_map/all_to_all | solution.py:131
  85.6 19.2 %all-to-all-start.1 = ((bf16[16,16,768]{2,1,0:T(8,128)(2,1)}), bf16[16,16,768]{2,1,0:T(8,128)(2,1)S(1)}, u32[]{:S(2)}, u32[]{:S(2)}) async-start(bf16[16,16,768]{2,1,0:T(8,128)(2,1)} %all-to-all-done), calls=%async_computation.1 | async-start | bytes 786432 | tf_op jit(solution)/shard_map/all_to_all | solution.py:135
  107.0 5.0 %all-to-all-done.1 = bf16[16,16,768]{2,1,0:T(8,128)(2,1)S(1)} async-done(((bf16[16,16,768]{2,1,0:T(8,128)(2,1)}), bf16[16,16,768]{2,1,0:T(8,128)(2,1)S(1)}, u32[]{:S(2)}, u32[]{:S(2)}) %all-to-all-start.1) | async-done | bytes 393248 | tf_op jit(solution)/shard_map/all_to_all | solution.py:135
  112.8 2.0 copy.110
  114.8 6.8 %all-to-all-start.2 = ((bf16[64,16,768]{2,1,0:T(8,128)(2,1)}), bf16[64,16,768]{2,1,0:T(8,128)(2,1)S(1)}, u32[]{:S(2)}, u32[]{:S(2)}) async-start(bf16[64,16,768]{2,1,0:T(8,128)(2,1)} %copy.110), calls=%async_computation.2 | async-start | bytes 3145728 | tf_op jit(solution)/shard_map/all_to_all | solution.py:159
  123.4 20.0 %all-to-all-done.2 = bf16[64,16,768]{2,1,0:T(8,128)(2,1)S(1)} async-done(((bf16[64,16,768]{2,1,0:T(8,128)(2,1)}), bf16[64,16,768]{2,1,0:T(8,128)(2,1)S(1)}, u32[]{:S(2)}, u32[]{:S(2)}) %all-to-all-start.2) | async-done | bytes 1572896 | tf_op jit(solution)/shard_map/all_to_all | solution.py:159
  147.3 1.2 fusion.98
  148.5 1.3 convolution_add_fusion
  149.8 3.0 %convolution_convert_fusion.3 = bf16[2,256,768]{2,1,0:T(8,128)(2,1)} fusion(bf16[2,256,768]{2,1,0:T(8,128)(2,1)S(1)} %squeeze.29, f32[2,256,256]{1,2,0:T(8,128)} %fusion.98, f32[2,256,256]{1,2,0:T(8,128)} %convolution_add_fusion, f32[2,256,256]{1,2,0:T(8,128)S(1)} %get-tuple-element.35, f32[2,256]{1,0:T(2,128)S(1)} %get-tuple-element.34, ...), kind=kOutput, calls=%fused_computation.11 | convolution fusion | flops 203293440 | bytes 3147784 | tf_op jit(solution)/shard_map/vmap()/dot_general | solution.py:16
  152.8 1.8 convolution_convert_fusion.2
  154.6 1.7 stack.37
  156.8 0.9 copy.123
  157.7 27.9 %all_to_all.30 = bf16[64,16,768]{2,1,0:T(8,128)(2,1)S(1)} all-to-all(bf16[64,16,768]{2,1,0:T(8,128)(2,1)S(1)} %copy.123), channel_id=1, replica_groups={{0,1,2,3,64,65,66,67,128,129,130,131,192,193,194,195,256,257,258,259,32..., dimensions={0} | all-to-all | bytes 3145728 | tf_op jit(solution)/shard_map/all_to_all | solution.py:174
  186.2 1.1 fusion.115
  188.2 13.9 %all_to_all.31 = bf16[16,16,768]{2,1,0:T(8,128)(2,1)} all-to-all(bf16[16,16,768]{2,1,0:T(8,128)(2,1)S(1)} %reshape.488), channel_id=1, replica_groups={{0,64,128,192,256,320,384,448,512,576,640,704,768,832,896,960},{1,65,12..., dimensions={0} | all-to-all | bytes 786432 | tf_op jit(solution)/shard_map/all_to_all | solution.py:183
  202.1 22.5 %all-to-all-start.5 = ((bf16[16,16,768]{2,1,0:T(8,128)(2,1)}), bf16[16,16,768]{2,1,0:T(8,128)(2,1)S(1)}, u32[]{:S(2)}, u32[]{:S(2)}) async-start(bf16[16,16,768]{2,1,0:T(8,128)(2,1)} %all_to_all.31), calls=%async_computation.5 | async-start | bytes 786432 | tf_op jit(solution)/shard_map/all_to_all | solution.py:185
  225.6 13.8 %collective-permute-start.1 = (bf16[72,768]{1,0:T(8,128)(2,1)S(1)}, bf16[72,768]{1,0:T(8,128)(2,1)S(1)}, u32[]{:S(2)}, u32[]{:S(2)}) collective-permute-start(bf16[72,768]{1,0:T(8,128)(2,1)S(1)} %pad_maximum_fusion.3), channel_id=1, source_target_pairs={{0,0},{1,1},{2,2},{3,3},{64,4},{65,5},{66,6},{67,7},{128,8},{129,9... | collective-permute-start | bytes 331784 | tf_op jit(solution)/shard_map/ppermute | solution.py:180
  239.4 38.8 %collective-permute-done.1 = bf16[72,768]{1,0:T(8,128)(2,1)S(1)} collective-permute-done((bf16[72,768]{1,0:T(8,128)(2,1)S(1)}, bf16[72,768]{1,0:T(8,128)(2,1)S(1)}, u32[]{:S(2)}, u32[]{:S(2)}) %collective-permute-start.1) | collective-permute-done | bytes 110624 | tf_op jit(solution)/shard_map/ppermute | solution.py:180
  (90 shorter events, 15.4 us)
Async XLA Ops:
  0.6 121.4 %copy-start = (s32[256]{0:T(256)S(1)}, s32[256]{0:T(256)}, u32[]{:S(2)}) copy-start(s32[256]{0:T(256)} %param.7) | copy-start | bytes 3076
  0.6 33.3 %copy-start.1 = (bf16[16,4,768]{2,1,0:T(4,128)(2,1)S(1)}, bf16[16,4,768]{2,1,0:T(4,128)(2,1)}, u32[]{:S(2)}) copy-start(bf16[16,4,768]{2,1,0:T(4,128)(2,1)} %param.6) | copy-start | bytes 294916
  2.2 31.9 %copy-start.2 = (f32[2]{0:T(128)S(1)}, f32[2]{0:T(128)}, u32[]{:S(2)}) copy-start(f32[2]{0:T(128)} %param.9) | copy-start | bytes 28
  5.4 80.2 %all-to-all-start = ((bf16[16,16,768]{2,1,0:T(8,128)(2,1)}), bf16[16,16,768]{2,1,0:T(8,128)(2,1)}, u32[]{:S(2)}, u32[]{:S(2)}) async-start(bf16[16,16,768]{2,1,0:T(8,128)(2,1)} %reshape.481), calls=%async_computation | async-start | bytes 786432 | tf_op jit(solution)/shard_map/all_to_all | solution.py:131
  34.2 72.3 %collective-permute-start = (bf16[72,768]{1,0:T(8,128)(2,1)S(1)}, bf16[72,768]{1,0:T(8,128)(2,1)S(1)}, u32[]{:S(2)}, u32[]{:S(2)}) collective-permute-start(bf16[72,768]{1,0:T(8,128)(2,1)S(1)} %pad_maximum_fusion.2), channel_id=1, source_target_pairs={{0,0},{1,1},{2,2},{3,3},{4,64},{5,65},{6,66},{7,67},{8,128},{9,129... | collective-permute-start | bytes 331784 | tf_op jit(solution)/shard_map/ppermute | solution.py:134
  85.6 26.3 %all-to-all-start.1 = ((bf16[16,16,768]{2,1,0:T(8,128)(2,1)}), bf16[16,16,768]{2,1,0:T(8,128)(2,1)S(1)}, u32[]{:S(2)}, u32[]{:S(2)}) async-start(bf16[16,16,768]{2,1,0:T(8,128)(2,1)} %all-to-all-done), calls=%async_computation.1 | async-start | bytes 786432 | tf_op jit(solution)/shard_map/all_to_all | solution.py:135
  114.8 28.6 %all-to-all-start.2 = ((bf16[64,16,768]{2,1,0:T(8,128)(2,1)}), bf16[64,16,768]{2,1,0:T(8,128)(2,1)S(1)}, u32[]{:S(2)}, u32[]{:S(2)}) async-start(bf16[64,16,768]{2,1,0:T(8,128)(2,1)} %copy.110), calls=%async_computation.2 | async-start | bytes 3145728 | tf_op jit(solution)/shard_map/all_to_all | solution.py:159
  149.8 3.0 %copy-start.3 = (f32[2,256,256]{1,2,0:T(8,128)S(1)}, f32[2,256,256]{1,2,0:T(8,128)}, u32[]{:S(2)}) copy-start(f32[2,256,256]{1,2,0:T(8,128)} %fusion.98) | copy-start | bytes 1572868
  202.1 76.8 %all-to-all-start.5 = ((bf16[16,16,768]{2,1,0:T(8,128)(2,1)}), bf16[16,16,768]{2,1,0:T(8,128)(2,1)S(1)}, u32[]{:S(2)}, u32[]{:S(2)}) async-start(bf16[16,16,768]{2,1,0:T(8,128)(2,1)} %all_to_all.31), calls=%async_computation.5 | async-start | bytes 786432 | tf_op jit(solution)/shard_map/all_to_all | solution.py:185
  225.6 52.6 %collective-permute-start.1 = (bf16[72,768]{1,0:T(8,128)(2,1)S(1)}, bf16[72,768]{1,0:T(8,128)(2,1)S(1)}, u32[]{:S(2)}, u32[]{:S(2)}) collective-permute-start(bf16[72,768]{1,0:T(8,128)(2,1)S(1)} %pad_maximum_fusion.3), channel_id=1, source_target_pairs={{0,0},{1,1},{2,2},{3,3},{64,4},{65,5},{66,6},{67,7},{128,8},{129,9... | collective-permute-start | bytes 331784 | tf_op jit(solution)/shard_map/ppermute | solution.py:180

commit v3 on v2

v3 whole, which is shorter than its diff:
```python
import functools
import math

import jax
import jax.numpy as jnp
from jax import lax
from jax.experimental import pallas as pl
from jax.experimental.pallas import tpu as pltpu
from jax.sharding import PartitionSpec as P

score_scale = 2.0
spread_floor = 1.0
log_weight = 0.1
epsilon = 1e-06
slots = 4


def dot(left, right, contract, out=jnp.float32):
    return lax.dot_general(left, right, (contract, ((), ())), preferred_element_type=out)


def split(values, parts):
    pieces = []
    for _ in range(parts):
        piece = lax.reduce_precision(values, 8, 7)
        pieces.append(piece.astype(jnp.bfloat16))
        values = values - piece
    return pieces


def with_scalars(rows, scalars):
    pieces = jnp.stack(split(scalars, 3))
    pad = ((0, 8 - pieces.shape[0]), (0, rows.shape[1] - pieces.shape[1]))
    return jnp.concatenate([rows, jnp.pad(pieces, pad)], axis=0)


def without_scalars(packed, count):
    pieces = packed[-8:-5, :count].astype(jnp.float32)
    return packed[:-8], (pieces[0] + pieces[1]) + pieces[2]


def pair_math(n_first, n_partner, len_first, len_partner, weight, row_time, column_time):
    factor = score_scale / math.sqrt(n_first.shape[1])
    scores = dot(n_first, n_partner, ((1,), (1,))) * factor
    forward_exp = jnp.where(column_time < len_partner, jnp.exp(scores), 0.0)
    forward_prob = forward_exp / jnp.sum(forward_exp, axis=1, keepdims=True)
    prob = forward_prob.astype(jnp.bfloat16)
    high = scores.astype(jnp.bfloat16)
    low = (scores - high.astype(jnp.float32)).astype(jnp.bfloat16)
    backward_scores = dot(prob, high, ((1,), (1,))) + dot(prob, low, ((1,), (1,)))
    backward_exp = jnp.where(column_time < len_first, jnp.exp(backward_scores), 0.0)
    back_prob = backward_exp / jnp.sum(backward_exp, axis=1, keepdims=True)
    mean_time = jnp.sum(back_prob * column_time, axis=1, keepdims=True)
    offsets = column_time - mean_time
    squares = offsets * offsets
    variance = jnp.sum(back_prob * squares, axis=1, keepdims=True)
    spread = variance + spread_floor
    missed = row_time - mean_time
    ratio = missed / spread
    terms = missed * ratio + log_weight * jnp.log(spread)
    valid = row_time < len_first
    loss = jnp.sum(jnp.where(valid, terms, 0.0)) / len_first
    row_weight = jnp.where(valid, weight / len_first, 0.0)
    d_mean = -2.0 * ratio * row_weight
    d_spread = (log_weight / spread - ratio * ratio) * row_weight
    d_back = back_prob * (d_mean * offsets + d_spread * (squares - variance))
    d_low = d_back.astype(jnp.bfloat16)
    d_prob = dot(d_low, high, ((1,), (0,))) + dot(d_low, low, ((1,), (0,)))
    d_scores = forward_prob * (d_prob - jnp.sum(forward_prob * d_prob, axis=1, keepdims=True))
    d_scores = d_scores + dot(d_back.T.astype(jnp.bfloat16), prob, ((1,), (0,)))
    d_scores = d_scores * factor
    grad_first = dot(d_scores.astype(jnp.bfloat16), n_partner, ((1,), (0,)))
    grad_partner = dot(d_scores.T.astype(jnp.bfloat16), n_first, ((1,), (0,)))
    return loss, grad_first, grad_partner


def pair_kernel(block, weights, length_ref, weight_ref, rows_ref, out_ref, loss_ref, wide):
    total = rows_ref.shape[0]
    count = weights
    chunk = 2 * count * block
    sources = total // chunk
    frames = sources * block
    lanes = wide.shape[2]
    strips = wide.shape[0]
    for c in range(strips):
        wide[c] = rows_ref[:, c * lanes : (c + 1) * lanes].astype(jnp.float32)
    row = lax.broadcasted_iota(jnp.int32, (frames, 1), 0)
    row_time = ((row % sources) * block + row // sources).astype(jnp.float32)
    column = lax.broadcasted_iota(jnp.int32, (1, frames), 1)
    column_time = ((column % sources) * block + column // sources).astype(jnp.float32)

    def place(kind, pair, frame):
        return pl.ds((kind * count + pair) * block + frame, sources, stride=chunk)

    for pair in range(count):
        clips = [
            jnp.concatenate(
                [
                    jnp.concatenate(
                        [wide[c, place(kind, pair, f), :] for f in range(block)], axis=0
                    ).astype(jnp.bfloat16)
                    for c in range(strips)
                ],
                axis=1,
            )
            for kind in range(2)
        ]
        loss, *grads = pair_math(
            clips[0],
            clips[1],
            length_ref[0, pair].astype(jnp.float32),
            length_ref[1, pair].astype(jnp.float32),
            weight_ref[pair],
            row_time,
            column_time,
        )
        loss_ref[pair] = loss
        for kind in range(2):
            for f in range(block):
                part = grads[kind][f * sources : (f + 1) * sources]
                for c in range(strips):
                    wide[c, place(kind, pair, f), :] = part[:, c * lanes : (c + 1) * lanes]
    for c in range(strips):
        out_ref[:, c * lanes : (c + 1) * lanes] = wide[c].astype(jnp.bfloat16)


def pair_call(rows, lengths, weight, block):
    smem = pl.BlockSpec(memory_space=pltpu.SMEM)
    vmem = pl.BlockSpec(memory_space=pltpu.VMEM)
    return pl.pallas_call(
        functools.partial(pair_kernel, block, weight.shape[0]),
        out_shape=(
            jax.ShapeDtypeStruct(rows.shape, jnp.bfloat16),
            jax.ShapeDtypeStruct(weight.shape, jnp.float32),
        ),
        in_specs=[smem, smem, vmem],
        out_specs=(vmem, smem),
        scratch_shapes=[pltpu.VMEM((rows.shape[1] // 128, rows.shape[0], 128), jnp.float32)],
        compiler_params=pltpu.CompilerParams(vmem_limit_bytes=40 * 1024 * 1024),
    )(lengths, weight, rows)


def spread_rows(hot, block):
    rows = jnp.arange(hot.shape[0] * block, dtype=jnp.int32)
    columns = jnp.arange(hot.shape[1] * block, dtype=jnp.int32)
    same = rows[:, None] % block == columns[None, :] % block
    wide = jnp.repeat(jnp.repeat(hot, block, axis=0), block, axis=1)
    return jnp.where(same, wide, 0).astype(jnp.bfloat16)


def shards(embeddings, lengths, pairs, scaled_weight):
    owners = lax.axis_size("clip")
    times = lax.axis_size("tm")
    clip_count, block, feature = embeddings.shape
    per_device = scaled_weight.shape[0]
    per_owner = per_device * times
    row_width = block * feature
    spots = times // owners
    column = lax.axis_index("clip")
    time_index = lax.axis_index("tm")
    owner = time_index // spots
    spot = time_index % spots
    turn = (column - owner + owners) % owners
    place = turn * spots + spot

    long_range = [[a + spots * i for i in range(owners)] for a in range(spots)]
    home = [
        [((m + c) % owners) * times + spots * c + q for m in range(owners) for q in range(spots)]
        for c in range(owners)
    ]
    plane = [
        [((m + t // spots) % owners) * times + t for m in range(owners)] for t in range(times)
    ]
    swap = [
        (c * times + t, ((t // spots + c) % owners) * times + c * spots + t % spots)
        for c in range(owners)
        for t in range(times)
    ]
    back = [(there, here) for here, there in swap]
    both = ("clip", "tm")

    as_float = embeddings.astype(jnp.float32)
    scale = lax.rsqrt(jnp.mean(as_float * as_float, axis=-1, keepdims=True) + epsilon)
    normalized = (as_float * scale).astype(jnp.bfloat16).reshape(clip_count * block, feature)

    packed = with_scalars(normalized, scaled_weight)

    grouped = pairs.reshape(owners, per_owner, 2)
    clips = jnp.arange(owners * clip_count, dtype=jnp.int32)
    used = jnp.any(grouped[:, :, 1, None] == clips[None, None, :], axis=1)
    before = (clips[:, None] // clip_count == clips[None, :] // clip_count) & (
        clips[:, None] < clips[None, :]
    )
    rank = dot(used.astype(jnp.bfloat16), before.astype(jnp.bfloat16), ((1,), (0,)))
    rank = jnp.where(used, rank.astype(jnp.int32), -1)
    mine = lax.dynamic_slice_in_dim(rank, column * clip_count, clip_count, 1)
    slot_ids = jnp.arange(slots, dtype=jnp.int32)
    chosen = mine[:, None, :] == slot_ids[None, :, None]
    chosen = chosen.reshape(owners * slots, clip_count).astype(jnp.bfloat16)

    outgoing = dot(
        spread_rows(chosen, block), normalized, ((1,), (0,)), jnp.bfloat16
    ).reshape(owners, slots * block, feature)
    outgoing = lax.all_to_all(
        outgoing, "tm", 0, 0, axis_index_groups=long_range, tiled=True
    )
    firsts, weight = without_scalars(lax.ppermute(packed, both, swap), per_device)
    partners = lax.all_to_all(outgoing, both, 0, 0, axis_index_groups=plane, tiled=True)

    owned = lax.dynamic_index_in_dim(grouped, owner, 0, keepdims=False)
    owned_rank = lax.dynamic_index_in_dim(rank, owner, 0, keepdims=False)
    first_slot = owned[:, 0] - owner * clip_count
    partner_is = owned[:, 1][:, None] == clips[None, :]
    partner_slot = jnp.sum(jnp.where(partner_is, owned_rank[None, :], 0), axis=1)
    source = (owned[:, 1] // clip_count - owner + owners) % owners
    partner_slot = partner_slot + source * slots
    slot_of = jnp.stack(
        [first_slot.reshape(times, per_device), partner_slot.reshape(times, per_device)], axis=1
    ).reshape(-1)
    row_count = 2 * per_owner * block
    row_slot = jnp.repeat(slot_of, block)
    row_index = jnp.arange(row_count, dtype=jnp.int32)
    row_key = row_slot * block + row_index % block
    is_first = (row_index // (per_device * block)) % 2 == 0
    first_key = jnp.where(is_first, row_key, -1)
    partner_key = jnp.where(is_first, -1, row_key)
    first_spots = jnp.arange(clip_count * block, dtype=jnp.int32)
    partner_spots = jnp.arange(owners * slots * block, dtype=jnp.int32)
    first_hot = (first_key[:, None] == first_spots[None, :]).astype(jnp.bfloat16)
    partner_hot = (partner_key[:, None] == partner_spots[None, :]).astype(jnp.bfloat16)
    first_back = (first_spots[:, None] == first_key[None, :]).astype(jnp.bfloat16)
    partner_back = (partner_spots[:, None] == partner_key[None, :]).astype(jnp.bfloat16)

    rows = dot(first_hot, firsts, ((1,), (0,)))
    rows = rows + dot(partner_hot, partners.reshape(-1, feature), ((1,), (0,)))
    rows = rows.astype(jnp.bfloat16).reshape(times, 2 * per_device * block, feature)
    rows = lax.all_to_all(rows, both, 0, 0, axis_index_groups=home, tiled=True)

    my_ids = lax.dynamic_slice_in_dim(owned, place * per_device, per_device, 0)
    pair_lengths = jnp.take(lengths, my_ids.T)
    grads, losses = pair_call(rows.reshape(row_count, feature), pair_lengths, weight, block)

    grads = grads.reshape(times, 2 * per_device * block, feature)
    returned = lax.all_to_all(grads, both, 0, 0, axis_index_groups=home, tiled=True)
    returned = returned.reshape(row_count, feature)
    partner_sum = dot(partner_back, returned, ((1,), (0,))).astype(jnp.bfloat16)
    first_sum = dot(first_back, returned, ((1,), (0,))).astype(jnp.bfloat16)
    first_sum = with_scalars(first_sum, losses)
    first_sum = lax.ppermute(first_sum, both, back)
    partner_sum = partner_sum.reshape(owners, slots * block, feature)
    partner_sum = lax.all_to_all(partner_sum, both, 0, 0, axis_index_groups=plane, tiled=True)
    first_sum, losses = without_scalars(first_sum, per_device)
    partner_sum = lax.all_to_all(
        partner_sum, "tm", 0, 0, axis_index_groups=long_range, tiled=True
    )
    total = dot(spread_rows(chosen.T, block), partner_sum.reshape(-1, feature), ((1,), (0,)))
    total = (total + first_sum.astype(jnp.float32)).reshape(clip_count, block, feature)
    unit = as_float * scale
    gradient = scale * (total - unit * jnp.mean(total * unit, axis=-1, keepdims=True))
    return (losses, gradient.astype(jnp.bfloat16))


def solution(mesh):
    in_specs = (P("clip", "tm", None), P(), P(), P(("clip", "tm")))
    out_specs = (P(("clip", "tm")), P("clip", "tm", None))
    return jax.shard_map(shards, mesh=mesh, in_specs=in_specs, out_specs=out_specs, check_vma=False)
```

time: 285 us -> 275 us (0.965)
  local copies, waits for them, and re-layouts: 15.9 us -> 3.48 us
  matrix products: 11.3 us -> 4.9 us
  Pallas kernels: 0 us -> 5.72 us
    reshape x13 -> x5, local copies, waits for them, and re-layouts: 6.33 us -> 0.27 us  [the longest x2 0.16 us: spread_rows(): wide = jnp.repeat(jnp.repeat(hot, block, axis=0), block, axis=1)]
    dot_general x14 -> x7, matrix products: 10.8 us -> 4.9 us  [dot(): lax.dot_general(left, right, (contract, ((), ())), preferred_element_type...]
    pallas_call x0 -> x1, Pallas kernels: none -> 5.72 us  [pair_call(): pl.pallas_call(functools.partial(pair_kernel, block, weight.shape[0]), ou...]
where the time goes in v3:
time: 275 us; the launch traced here: 270 us
  waiting for transfers between devices  104 us (38%)
  starting transfers between devices  103 us (37%)
  blocking collectives  41.7 us (15%)
  Pallas kernels  5.72 us (2%)
  matrix products  4.9 us (2%)
  other arithmetic  4.85 us (2%)
  local copies, waits for them, and re-layouts  3.48 us (1%)
    ppermute x1, waiting for transfers between devices, shards(): first_sum = lax.ppermute(first_sum, both, back)  38.9 us
    all_to_all x1, waiting for transfers between devices, shards(): lax.all_to_all(outgoing, 'tm', 0, 0, axis_index_groups=long_range, tiled=...  38.5 us
    all_to_all x1, starting transfers between devices, shards(): lax.all_to_all(outgoing, 'tm', 0, 0, axis_index_groups=long_range, tiled=...  28.5 us
    all_to_all x1, blocking collectives, shards(): lax.all_to_all(grads, both, 0, 0, axis_index_groups=home, tiled=True)  27.9 us
    all_to_all x1, starting transfers between devices, shards(): lax.all_to_all(partner_sum, 'tm', 0, 0, axis_index_groups=long_range, til...  22.6 us
    all_to_all x1, waiting for transfers between devices, shards(): rows = lax.all_to_all(rows, both, 0, 0, axis_index_groups=home, tiled=True)  20.8 us
    all_to_all x1, starting transfers between devices, shards(): lax.all_to_all(outgoing, both, 0, 0, axis_index_groups=plane, tiled=True)  19.2 us
    all_to_all x1, blocking collectives, shards(): lax.all_to_all(partner_sum, both, 0, 0, axis_index_groups=plane, tiled=True)  13.9 us
  transfers between devices with their start and end apart: 6, of which 4 were waited for; matrix products, arithmetic and copies ran while one was open for 2% of the time, Pallas kernels for 0%

profile of v3, /device:TPU:24, one launch (start us, length us, event | category | flops | bytes accessed | tf_op | source)
XLA Modules:
  0.0 269.6 jit_solution(5582491519653456821)
XLA Ops:
  0.7 0.7 copy.53
  1.4 1.0 fusion.18
  2.4 1.0 fusion.13
  3.5 0.4 fusion
  4.8 1.0 fusion.5
  5.9 28.5 %all-to-all-start = ((bf16[16,16,768]{2,1,0:T(8,128)(2,1)}), bf16[16,16,768]{2,1,0:T(8,128)(2,1)}, u32[]{:S(2)}, u32[]{:S(2)}) async-start(bf16[16,16,768]{2,1,0:T(8,128)(2,1)} %fusion.5), calls=%async_computation | async-start | bytes 786432 | tf_op jit(solution)/shard_map/all_to_all | solution.py:204
  34.5 12.5 %collective-permute-start = (bf16[72,768]{1,0:T(8,128)(2,1)S(1)}, bf16[72,768]{1,0:T(8,128)(2,1)S(1)}, u32[]{:S(2)}, u32[]{:S(2)}) collective-permute-start(bf16[72,768]{1,0:T(8,128)(2,1)S(1)} %pad_maximum_fusion), channel_id=1, source_target_pairs={{0,0},{1,1},{2,2},{3,3},{4,64},{5,65},{6,66},{7,67},{8,128},{9,129... | collective-permute-start | bytes 331784 | tf_op jit(solution)/shard_map/ppermute | solution.py:207
  47.5 38.5 %all-to-all-done = bf16[16,16,768]{2,1,0:T(8,128)(2,1)} async-done(((bf16[16,16,768]{2,1,0:T(8,128)(2,1)}), bf16[16,16,768]{2,1,0:T(8,128)(2,1)}, u32[]{:S(2)}, u32[]{:S(2)}) %all-to-all-start) | async-done | bytes 393248 | tf_op jit(solution)/shard_map/all_to_all | solution.py:204
  86.1 19.2 %all-to-all-start.1 = ((bf16[16,16,768]{2,1,0:T(8,128)(2,1)}), bf16[16,16,768]{2,1,0:T(8,128)(2,1)S(1)}, u32[]{:S(2)}, u32[]{:S(2)}) async-start(bf16[16,16,768]{2,1,0:T(8,128)(2,1)} %all-to-all-done), calls=%async_computation.1 | async-start | bytes 786432 | tf_op jit(solution)/shard_map/all_to_all | solution.py:208
  106.2 6.2 %all-to-all-done.1 = bf16[16,16,768]{2,1,0:T(8,128)(2,1)S(1)} async-done(((bf16[16,16,768]{2,1,0:T(8,128)(2,1)}), bf16[16,16,768]{2,1,0:T(8,128)(2,1)S(1)}, u32[]{:S(2)}, u32[]{:S(2)}) %all-to-all-start.1) | async-done | bytes 393248 | tf_op jit(solution)/shard_map/all_to_all | solution.py:208
  112.4 0.6 fusion.2
  113.1 1.8 add_convert_fusion
  114.9 6.8 %all-to-all-start.2 = ((bf16[64,16,768]{2,1,0:T(8,128)(2,1)}), bf16[64,16,768]{2,1,0:T(8,128)(2,1)S(1)}, u32[]{:S(2)}, u32[]{:S(2)}) async-start(bf16[64,16,768]{2,1,0:T(8,128)(2,1)} %bitcast.13), calls=%async_computation.2 | async-start | bytes 3145728 | tf_op jit(solution)/shard_map/all_to_all | solution.py:237
  121.9 0.6 gather_fusion
  122.6 20.8 %all-to-all-done.2 = bf16[64,16,768]{2,1,0:T(8,128)(2,1)S(1)} async-done(((bf16[64,16,768]{2,1,0:T(8,128)(2,1)}), bf16[64,16,768]{2,1,0:T(8,128)(2,1)S(1)}, u32[]{:S(2)}, u32[]{:S(2)}) %all-to-all-start.2) | async-done | bytes 1572896 | tf_op jit(solution)/shard_map/all_to_all | solution.py:237
  143.5 5.7 %shard_map.59 = (bf16[1024,768]{1,0:T(8,128)(2,1)S(1)}, f32[2]{0:T(128)S(1)}) custom-call(s32[2,2]{1,0:T(2,128)S(1)} %and_select_fusion.2.length_ref, f32[2]{0:T(128)S(1)} %add_bitcast_fusion.1.weight_ref, bf16[1024,768]{1,0:T(8,128)(2,1)S(1)} %bitcast.56), custom_call_target="tpu_custom_call" | custom-call | tf_op jit(solution)/shard_map/pallas_call | solution.py:130
  149.2 27.9 %all_to_all.30 = bf16[64,16,768]{2,1,0:T(8,128)(2,1)S(1)} all-to-all(bf16[64,16,768]{2,1,0:T(8,128)(2,1)S(1)} %bitcast.57), channel_id=1, replica_groups={{0,1,2,3,64,65,66,67,128,129,130,131,192,193,194,195,256,257,258,259,32..., dimensions={0} | all-to-all | bytes 3145728 | tf_op jit(solution)/shard_map/all_to_all | solution.py:244
  177.0 0.6 convolution_convert_fusion
  177.7 13.9 %all_to_all.31 = bf16[16,16,768]{2,1,0:T(8,128)(2,1)} all-to-all(bf16[16,16,768]{2,1,0:T(8,128)(2,1)S(1)} %bitcast.62), channel_id=1, replica_groups={{0,64,128,192,256,320,384,448,512,576,640,704,768,832,896,960},{1,65,12..., dimensions={0} | all-to-all | bytes 786432 | tf_op jit(solution)/shard_map/all_to_all | solution.py:251
  191.6 22.6 %all-to-all-start.5 = ((bf16[16,16,768]{2,1,0:T(8,128)(2,1)}), bf16[16,16,768]{2,1,0:T(8,128)(2,1)S(1)}, u32[]{:S(2)}, u32[]{:S(2)}) async-start(bf16[16,16,768]{2,1,0:T(8,128)(2,1)} %all_to_all.31), calls=%async_computation.5 | async-start | bytes 786432 | tf_op jit(solution)/shard_map/all_to_all | solution.py:253
  214.9 13.8 %collective-permute-start.1 = (bf16[72,768]{1,0:T(8,128)(2,1)S(1)}, bf16[72,768]{1,0:T(8,128)(2,1)S(1)}, u32[]{:S(2)}, u32[]{:S(2)}) collective-permute-start(bf16[72,768]{1,0:T(8,128)(2,1)S(1)} %pad_maximum_fusion.1), channel_id=1, source_target_pairs={{0,0},{1,1},{2,2},{3,3},{64,4},{65,5},{66,6},{67,7},{128,8},{129,9... | collective-permute-start | bytes 331784 | tf_op jit(solution)/shard_map/ppermute | solution.py:249
  228.8 38.9 %collective-permute-done.1 = bf16[72,768]{1,0:T(8,128)(2,1)S(1)} collective-permute-done((bf16[72,768]{1,0:T(8,128)(2,1)S(1)}, bf16[72,768]{1,0:T(8,128)(2,1)S(1)}, u32[]{:S(2)}, u32[]{:S(2)}) %collective-permute-start.1) | collective-permute-done | bytes 110624 | tf_op jit(solution)/shard_map/ppermute | solution.py:249
  267.7 0.5 add_bitcast_fusion
  268.8 0.9 fusion.17
  (67 shorter events, 4.0 us)
Async XLA Ops:
  0.6 121.3 %copy-start = (s32[256]{0:T(256)S(1)}, s32[256]{0:T(256)}, u32[]{:S(2)}) copy-start(s32[256]{0:T(256)} %param.5) | copy-start | bytes 3076
  1.4 33.0 %copy-start.2 = (f32[2]{0:T(128)S(1)}, f32[2]{0:T(128)}, u32[]{:S(2)}) copy-start(f32[2]{0:T(128)} %param.7) | copy-start | bytes 28
  5.9 80.2 %all-to-all-start = ((bf16[16,16,768]{2,1,0:T(8,128)(2,1)}), bf16[16,16,768]{2,1,0:T(8,128)(2,1)}, u32[]{:S(2)}, u32[]{:S(2)}) async-start(bf16[16,16,768]{2,1,0:T(8,128)(2,1)} %fusion.5), calls=%async_computation | async-start | bytes 786432 | tf_op jit(solution)/shard_map/all_to_all | solution.py:204
  34.5 78.6 %collective-permute-start = (bf16[72,768]{1,0:T(8,128)(2,1)S(1)}, bf16[72,768]{1,0:T(8,128)(2,1)S(1)}, u32[]{:S(2)}, u32[]{:S(2)}) collective-permute-start(bf16[72,768]{1,0:T(8,128)(2,1)S(1)} %pad_maximum_fusion), channel_id=1, source_target_pairs={{0,0},{1,1},{2,2},{3,3},{4,64},{5,65},{6,66},{7,67},{8,128},{9,129... | collective-permute-start | bytes 331784 | tf_op jit(solution)/shard_map/ppermute | solution.py:207
  86.1 26.3 %all-to-all-start.1 = ((bf16[16,16,768]{2,1,0:T(8,128)(2,1)}), bf16[16,16,768]{2,1,0:T(8,128)(2,1)S(1)}, u32[]{:S(2)}, u32[]{:S(2)}) async-start(bf16[16,16,768]{2,1,0:T(8,128)(2,1)} %all-to-all-done), calls=%async_computation.1 | async-start | bytes 786432 | tf_op jit(solution)/shard_map/all_to_all | solution.py:208
  114.9 28.6 %all-to-all-start.2 = ((bf16[64,16,768]{2,1,0:T(8,128)(2,1)}), bf16[64,16,768]{2,1,0:T(8,128)(2,1)S(1)}, u32[]{:S(2)}, u32[]{:S(2)}) async-start(bf16[64,16,768]{2,1,0:T(8,128)(2,1)} %bitcast.13), calls=%async_computation.2 | async-start | bytes 3145728 | tf_op jit(solution)/shard_map/all_to_all | solution.py:237
  191.6 76.7 %all-to-all-start.5 = ((bf16[16,16,768]{2,1,0:T(8,128)(2,1)}), bf16[16,16,768]{2,1,0:T(8,128)(2,1)S(1)}, u32[]{:S(2)}, u32[]{:S(2)}) async-start(bf16[16,16,768]{2,1,0:T(8,128)(2,1)} %all_to_all.31), calls=%async_computation.5 | async-start | bytes 786432 | tf_op jit(solution)/shard_map/all_to_all | solution.py:253
  214.5 54.1 %copy-start.1 = (bf16[16,4,768]{2,1,0:T(4,128)(2,1)S(1)}, bf16[16,4,768]{2,1,0:T(4,128)(2,1)}, u32[]{:S(2)}) copy-start(bf16[16,4,768]{2,1,0:T(4,128)(2,1)} %param.4) | copy-start | bytes 294916
  214.9 52.8 %collective-permute-start.1 = (bf16[72,768]{1,0:T(8,128)(2,1)S(1)}, bf16[72,768]{1,0:T(8,128)(2,1)S(1)}, u32[]{:S(2)}, u32[]{:S(2)}) collective-permute-start(bf16[72,768]{1,0:T(8,128)(2,1)S(1)} %pad_maximum_fusion.1), channel_id=1, source_target_pairs={{0,0},{1,1},{2,2},{3,3},{64,4},{65,5},{66,6},{67,7},{128,8},{129,9... | collective-permute-start | bytes 331784 | tf_op jit(solution)/shard_map/ppermute | solution.py:249

commit v4 on v3

--- a/solution.py
+++ b/solution.py
@@ -183,7 +183,11 @@
     scale = lax.rsqrt(jnp.mean(as_float * as_float, axis=-1, keepdims=True) + epsilon)
     normalized = (as_float * scale).astype(jnp.bfloat16).reshape(clip_count * block, feature)
 
-    packed = with_scalars(normalized, scaled_weight)
+    spread = lax.all_to_all(
+        normalized.reshape(clip_count, block, feature), "clip", 0, 0, tiled=True
+    ).reshape(clip_count * block, feature)
+    weight = lax.ppermute(scaled_weight, both, swap)
+    spread, weight = lax.optimization_barrier((spread, weight))
 
     grouped = pairs.reshape(owners, per_owner, 2)
     clips = jnp.arange(owners * clip_count, dtype=jnp.int32)
@@ -198,14 +202,34 @@
     chosen = mine[:, None, :] == slot_ids[None, :, None]
     chosen = chosen.reshape(owners * slots, clip_count).astype(jnp.bfloat16)
 
-    outgoing = dot(
-        spread_rows(chosen, block), normalized, ((1,), (0,)), jnp.bfloat16
-    ).reshape(owners, slots * block, feature)
+    depth = (slots + 1) * block
+    half = feature // 2
+    own = jnp.where(jnp.eye(owners, dtype=bool), slots, -1)
+    wanted = jnp.concatenate([mine, own], axis=1).astype(jnp.bfloat16)
+    out_row = jnp.arange(owners * 2 * depth, dtype=jnp.int32)
+    in_row = jnp.arange(2 * clip_count * block, dtype=jnp.int32)
+    of_owner = out_row[:, None] // (2 * depth) == jnp.arange(owners, dtype=jnp.int32)[None, :]
+    of_source = jnp.arange(2 * clip_count, dtype=jnp.int32)[:, None] == in_row[None, :] // block
+    wanted = dot(of_owner.astype(jnp.bfloat16), wanted, ((1,), (0,)), jnp.bfloat16)
+    wanted = dot(wanted, of_source.astype(jnp.bfloat16), ((1,), (0,))).astype(jnp.int32)
+    out_depth = out_row % depth
+    picked = (wanted == out_depth[:, None] // block) & (
+        out_depth[:, None] % block == in_row[None, :] % block
+    )
+    picked = picked.astype(jnp.bfloat16)
+    sources = jnp.concatenate([normalized, spread], axis=0)
+    upper = (out_row % (2 * depth) >= depth)[:, None]
+    outgoing = jnp.where(
+        upper,
+        dot(picked, sources[:, half:], ((1,), (0,))),
+        dot(picked, sources[:, :half], ((1,), (0,))),
+    )
+    outgoing = outgoing.astype(jnp.bfloat16).reshape(owners, 2 * depth, half)
     outgoing = lax.all_to_all(
         outgoing, "tm", 0, 0, axis_index_groups=long_range, tiled=True
     )
-    firsts, weight = without_scalars(lax.ppermute(packed, both, swap), per_device)
     partners = lax.all_to_all(outgoing, both, 0, 0, axis_index_groups=plane, tiled=True)
+    partners = partners.reshape(owners * 2 * depth, half)
 
     owned = lax.dynamic_index_in_dim(grouped, owner, 0, keepdims=False)
     owned_rank = lax.dynamic_index_in_dim(rank, owner, 0, keepdims=False)
@@ -226,13 +250,22 @@
     partner_key = jnp.where(is_first, -1, row_key)
     first_spots = jnp.arange(clip_count * block, dtype=jnp.int32)
     partner_spots = jnp.arange(owners * slots * block, dtype=jnp.int32)
-    first_hot = (first_key[:, None] == first_spots[None, :]).astype(jnp.bfloat16)
-    partner_hot = (partner_key[:, None] == partner_spots[None, :]).astype(jnp.bfloat16)
     first_back = (first_spots[:, None] == first_key[None, :]).astype(jnp.bfloat16)
     partner_back = (partner_spots[:, None] == partner_key[None, :]).astype(jnp.bfloat16)
 
-    rows = dot(first_hot, firsts, ((1,), (0,)))
-    rows = rows + dot(partner_hot, partners.reshape(-1, feature), ((1,), (0,)))
+    first_source = (first_slot - owner + owners * clip_count) % owners
+    entry_of = jnp.stack(
+        [
+            (first_source * 2 * depth + slots * block).reshape(times, per_device),
+            (source * 2 * depth + (partner_slot % slots) * block).reshape(times, per_device),
+        ],
+        axis=1,
+    ).reshape(-1)
+    entry = (jnp.repeat(entry_of, block) + row_index % block)[:, None]
+    entries = jnp.arange(owners * 2 * depth, dtype=jnp.int32)[None, :]
+    lower_rows = dot((entry == entries).astype(jnp.bfloat16), partners, ((1,), (0,)))
+    upper_rows = dot((entry + depth == entries).astype(jnp.bfloat16), partners, ((1,), (0,)))
+    rows = jnp.concatenate([lower_rows, upper_rows], axis=1)
     rows = rows.astype(jnp.bfloat16).reshape(times, 2 * per_device * block, feature)
     rows = lax.all_to_all(rows, both, 0, 0, axis_index_groups=home, tiled=True)
 

time: 275 us -> 283 us (1.029)
  waiting for transfers between devices: 104 us -> 133 us
  blocking collectives: 41.7 us -> 13.9 us
  starting transfers between devices: 103 us -> 106 us
    all_to_all x1 -> x0, blocking collectives: 27.9 us -> none  [shards(): lax.all_to_all(grads, both, 0, 0, axis_index_groups=home, tiled=True)]
    all_to_all x0 -> x2, starting transfers between devices: none -> 23.2 us  [the longest x1 16.2 us: shards(): lax.all_to_all(normalized.reshape(clip_count, block, feature), 'clip', 0,...]
    all_to_all x0 -> x2, waiting for transfers between devices: none -> 21.3 us  [the longest x1 21.3 us: shards(): lax.all_to_all(grads, both, 0, 0, axis_index_groups=home, tiled=True)]
    all_to_all x1, starting transfers between devices: 22.6 us -> 7.99 us  [shards(): lax.all_to_all(partner_sum, 'tm', 0, 0, axis_index_groups=long_range, til...]
    all_to_all x1, starting transfers between devices: 19.2 us -> 6.99 us  [shards(): lax.all_to_all(outgoing, both, 0, 0, axis_index_groups=plane, tiled=True)]
    all_to_all x1, waiting for transfers between devices: 38.5 us -> 45.7 us  [shards(): lax.all_to_all(outgoing, 'tm', 0, 0, axis_index_groups=long_range, tiled=...]
    all_to_all x1, starting transfers between devices: 6.8 us -> 13.4 us  [shards(): rows = lax.all_to_all(rows, both, 0, 0, axis_index_groups=home, tiled=True)]
  transfers between devices with their start and end apart: 6 -> 8, of which waited for: 4 -> 5; matrix products, arithmetic and copies ran while one was open for 2% -> 3% of each run, Pallas kernels for 0% -> 0%
where the time goes in v4:
time: 283 us; the launch traced here: 278 us
  waiting for transfers between devices  133 us (47%)
  starting transfers between devices  106 us (37%)
  blocking collectives  13.9 us (5%)
  Pallas kernels  6.87 us (2%)
  other arithmetic  6.68 us (2%)
  matrix products  5.28 us (2%)
  local copies, waits for them, and re-layouts  4.23 us (1%)
    all_to_all x1, waiting for transfers between devices, shards(): lax.all_to_all(outgoing, 'tm', 0, 0, axis_index_groups=long_range, tiled=...  45.7 us
    ppermute x1, waiting for transfers between devices, shards(): first_sum = lax.ppermute(first_sum, both, back)  38.2 us
    all_to_all x1, starting transfers between devices, shards(): lax.all_to_all(outgoing, 'tm', 0, 0, axis_index_groups=long_range, tiled=...  26.6 us
    all_to_all x1, waiting for transfers between devices, shards(): lax.all_to_all(grads, both, 0, 0, axis_index_groups=home, tiled=True)  21.3 us
    all_to_all x1, waiting for transfers between devices, shards(): rows = lax.all_to_all(rows, both, 0, 0, axis_index_groups=home, tiled=True)  20.8 us
    all_to_all x1, starting transfers between devices, shards(): lax.all_to_all(normalized.reshape(clip_count, block, feature), 'clip', 0,...  16.2 us
    ppermute x1, starting transfers between devices, shards(): first_sum = lax.ppermute(first_sum, both, back)  14.3 us
    ppermute x1, starting transfers between devices, shards(): weight = lax.ppermute(scaled_weight, both, swap)  13.9 us
  transfers between devices with their start and end apart: 8, of which 5 were waited for; matrix products, arithmetic and copies ran while one was open for 3% of the time, Pallas kernels for 0%

profile of v4, /device:TPU:24, one launch (start us, length us, event | category | flops | bytes accessed | tf_op | source)
XLA Modules:
  0.0 277.9 jit_solution(16086266870817313962)
XLA Ops:
  0.6 1.0 fusion.32
  1.7 1.6 fusion.27
  3.3 16.2 %all-to-all-start = ((bf16[16,4,768]{2,1,0:T(4,128)(2,1)}), bf16[16,4,768]{2,1,0:T(4,128)(2,1)S(1)}, u32[]{:S(2)}, u32[]{:S(2)}) async-start(bf16[16,4,768]{2,1,0:T(4,128)(2,1)} %fusion.27), calls=%async_computation | async-start | bytes 196608 | tf_op jit(solution)/shard_map/all_to_all | solution.py:186
  19.6 13.9 %collective-permute-start = (f32[2]{0:T(128)}, f32[2]{0:T(128)S(1)}, u32[]{:S(2)}, u32[]{:S(2)}) collective-permute-start(f32[2]{0:T(128)} %param.7), channel_id=1, source_target_pairs={{0,0},{1,1},{2,2},{3,3},{4,64},{5,65},{6,66},{7,67},{8,128},{9,129... | collective-permute-start | bytes 32 | tf_op jit(solution)/shard_map/ppermute | solution.py:189
  33.5 0.9 reshape.725
  34.5 0.7 copy.63
  36.9 1.1 fusion.15
  38.0 26.6 %all-to-all-start.1 = ((bf16[16,40,384]{2,1,0:T(8,128)(2,1)}), bf16[16,40,384]{2,1,0:T(8,128)(2,1)}, u32[]{:S(2)}, u32[]{:S(2)}) async-start(bf16[16,40,384]{2,1,0:T(8,128)(2,1)} %bitcast.9), calls=%async_computation.1 | async-start | bytes 983040 | tf_op jit(solution)/shard_map/all_to_all | solution.py:228
  65.5 45.7 %all-to-all-done.1 = bf16[16,40,384]{2,1,0:T(8,128)(2,1)} async-done(((bf16[16,40,384]{2,1,0:T(8,128)(2,1)}), bf16[16,40,384]{2,1,0:T(8,128)(2,1)}, u32[]{:S(2)}, u32[]{:S(2)}) %all-to-all-start.1) | async-done | bytes 491552 | tf_op jit(solution)/shard_map/all_to_all | solution.py:228
  111.2 7.0 %all-to-all-start.2 = ((bf16[16,40,384]{2,1,0:T(8,128)(2,1)}), bf16[16,40,384]{2,1,0:T(8,128)(2,1)S(1)}, u32[]{:S(2)}, u32[]{:S(2)}) async-start(bf16[16,40,384]{2,1,0:T(8,128)(2,1)} %all-to-all-done.1), calls=%async_computation.2 | async-start | bytes 983040 | tf_op jit(solution)/shard_map/all_to_all | solution.py:231
  118.5 7.5 %all-to-all-done.2 = bf16[16,40,384]{2,1,0:T(8,128)(2,1)S(1)} async-done(((bf16[16,40,384]{2,1,0:T(8,128)(2,1)}), bf16[16,40,384]{2,1,0:T(8,128)(2,1)S(1)}, u32[]{:S(2)}, u32[]{:S(2)}) %all-to-all-start.2) | async-done | bytes 491552 | tf_op jit(solution)/shard_map/all_to_all | solution.py:231
  125.9 1.0 fusion.7
  126.9 1.0 fusion.10
  127.8 1.3 pad_maximum_fusion
  129.1 13.4 %all-to-all-start.3 = ((bf16[64,16,768]{2,1,0:T(8,128)(2,1)}), bf16[64,16,768]{2,1,0:T(8,128)(2,1)S(1)}, u32[]{:S(2)}, u32[]{:S(2)}) async-start(bf16[64,16,768]{2,1,0:T(8,128)(2,1)} %pad_maximum_fusion), calls=%async_computation.3 | async-start | bytes 3145728 | tf_op jit(solution)/shard_map/all_to_all | solution.py:270
  143.5 20.8 %all-to-all-done.3 = bf16[64,16,768]{2,1,0:T(8,128)(2,1)S(1)} async-done(((bf16[64,16,768]{2,1,0:T(8,128)(2,1)}), bf16[64,16,768]{2,1,0:T(8,128)(2,1)S(1)}, u32[]{:S(2)}, u32[]{:S(2)}) %all-to-all-start.3) | async-done | bytes 1572896 | tf_op jit(solution)/shard_map/all_to_all | solution.py:270
  164.3 6.9 %shard_map.59 = (bf16[1024,768]{1,0:T(8,128)(2,1)}, f32[2]{0:T(128)S(1)}) custom-call(s32[2,2]{1,0:T(2,128)S(1)} %and_select_fusion.5.length_ref, f32[2]{0:T(128)S(1)} %collective-permute-done.weight_ref, bf16[1024,768]{1,0:T(8,128)(2,1)S(1)} %bitcast.61), custom_call_target="tpu_custom_call" | custom-call | tf_op jit(solution)/shard_map/pallas_call | solution.py:130
  171.2 6.9 %all-to-all-start.4 = ((bf16[64,16,768]{2,1,0:T(8,128)(2,1)}), bf16[64,16,768]{2,1,0:T(8,128)(2,1)S(1)}, u32[]{:S(2)}, u32[]{:S(2)}) async-start(bf16[64,16,768]{2,1,0:T(8,128)(2,1)} %bitcast.15), calls=%async_computation.4 | async-start | bytes 3145728 | tf_op jit(solution)/shard_map/all_to_all | solution.py:277
  178.6 21.3 %all-to-all-done.4 = bf16[64,16,768]{2,1,0:T(8,128)(2,1)S(1)} async-done(((bf16[64,16,768]{2,1,0:T(8,128)(2,1)}), bf16[64,16,768]{2,1,0:T(8,128)(2,1)S(1)}, u32[]{:S(2)}, u32[]{:S(2)}) %all-to-all-start.4) | async-done | bytes 1572896 | tf_op jit(solution)/shard_map/all_to_all | solution.py:277
  200.5 13.9 %all_to_all.35 = bf16[16,16,768]{2,1,0:T(8,128)(2,1)} all-to-all(bf16[16,16,768]{2,1,0:T(8,128)(2,1)S(1)} %bitcast.67), channel_id=1, replica_groups={{0,64,128,192,256,320,384,448,512,576,640,704,768,832,896,960},{1,65,12..., dimensions={0} | all-to-all | bytes 786432 | tf_op jit(solution)/shard_map/all_to_all | solution.py:284
  214.4 8.0 %all-to-all-start.6 = ((bf16[16,16,768]{2,1,0:T(8,128)(2,1)}), bf16[16,16,768]{2,1,0:T(8,128)(2,1)S(1)}, u32[]{:S(2)}, u32[]{:S(2)}) async-start(bf16[16,16,768]{2,1,0:T(8,128)(2,1)} %all_to_all.35), calls=%async_computation.6 | async-start | bytes 786432 | tf_op jit(solution)/shard_map/all_to_all | solution.py:286
  223.3 14.3 %collective-permute-start.1 = (bf16[72,768]{1,0:T(8,128)(2,1)S(1)}, bf16[72,768]{1,0:T(8,128)(2,1)S(1)}, u32[]{:S(2)}, u32[]{:S(2)}) collective-permute-start(bf16[72,768]{1,0:T(8,128)(2,1)S(1)} %pad_maximum_fusion.1), channel_id=1, source_target_pairs={{0,0},{1,1},{2,2},{3,3},{64,4},{65,5},{66,6},{67,7},{128,8},{129,9... | collective-permute-start | bytes 331784 | tf_op jit(solution)/shard_map/ppermute | solution.py:282
  237.8 38.2 %collective-permute-done.1 = bf16[72,768]{1,0:T(8,128)(2,1)S(1)} collective-permute-done((bf16[72,768]{1,0:T(8,128)(2,1)S(1)}, bf16[72,768]{1,0:T(8,128)(2,1)S(1)}, u32[]{:S(2)}, u32[]{:S(2)}) %collective-permute-start.1) | collective-permute-done | bytes 110624 | tf_op jit(solution)/shard_map/ppermute | solution.py:282
  277.0 0.9 fusion.31
  (73 shorter events, 6.7 us)
Async XLA Ops:
  0.6 142.1 %copy-start = (s32[256]{0:T(256)S(1)}, s32[256]{0:T(256)}, u32[]{:S(2)}) copy-start(s32[256]{0:T(256)} %param.5) | copy-start | bytes 3076
  3.3 33.2 %all-to-all-start = ((bf16[16,4,768]{2,1,0:T(4,128)(2,1)}), bf16[16,4,768]{2,1,0:T(4,128)(2,1)S(1)}, u32[]{:S(2)}, u32[]{:S(2)}) async-start(bf16[16,4,768]{2,1,0:T(4,128)(2,1)} %fusion.27), calls=%async_computation | async-start | bytes 196608 | tf_op jit(solution)/shard_map/all_to_all | solution.py:186
  19.6 17.0 %collective-permute-start = (f32[2]{0:T(128)}, f32[2]{0:T(128)S(1)}, u32[]{:S(2)}, u32[]{:S(2)}) collective-permute-start(f32[2]{0:T(128)} %param.7), channel_id=1, source_target_pairs={{0,0},{1,1},{2,2},{3,3},{4,64},{5,65},{6,66},{7,67},{8,128},{9,129... | collective-permute-start | bytes 32 | tf_op jit(solution)/shard_map/ppermute | solution.py:189
  38.0 73.3 %all-to-all-start.1 = ((bf16[16,40,384]{2,1,0:T(8,128)(2,1)}), bf16[16,40,384]{2,1,0:T(8,128)(2,1)}, u32[]{:S(2)}, u32[]{:S(2)}) async-start(bf16[16,40,384]{2,1,0:T(8,128)(2,1)} %bitcast.9), calls=%async_computation.1 | async-start | bytes 983040 | tf_op jit(solution)/shard_map/all_to_all | solution.py:228
  111.2 14.7 %all-to-all-start.2 = ((bf16[16,40,384]{2,1,0:T(8,128)(2,1)}), bf16[16,40,384]{2,1,0:T(8,128)(2,1)S(1)}, u32[]{:S(2)}, u32[]{:S(2)}) async-start(bf16[16,40,384]{2,1,0:T(8,128)(2,1)} %all-to-all-done.1), calls=%async_computation.2 | async-start | bytes 983040 | tf_op jit(solution)/shard_map/all_to_all | solution.py:231
  129.1 35.2 %all-to-all-start.3 = ((bf16[64,16,768]{2,1,0:T(8,128)(2,1)}), bf16[64,16,768]{2,1,0:T(8,128)(2,1)S(1)}, u32[]{:S(2)}, u32[]{:S(2)}) async-start(bf16[64,16,768]{2,1,0:T(8,128)(2,1)} %pad_maximum_fusion), calls=%async_computation.3 | async-start | bytes 3145728 | tf_op jit(solution)/shard_map/all_to_all | solution.py:270
  171.2 28.7 %all-to-all-start.4 = ((bf16[64,16,768]{2,1,0:T(8,128)(2,1)}), bf16[64,16,768]{2,1,0:T(8,128)(2,1)S(1)}, u32[]{:S(2)}, u32[]{:S(2)}) async-start(bf16[64,16,768]{2,1,0:T(8,128)(2,1)} %bitcast.15), calls=%async_computation.4 | async-start | bytes 3145728 | tf_op jit(solution)/shard_map/all_to_all | solution.py:277
  214.4 62.1 %all-to-all-start.6 = ((bf16[16,16,768]{2,1,0:T(8,128)(2,1)}), bf16[16,16,768]{2,1,0:T(8,128)(2,1)S(1)}, u32[]{:S(2)}, u32[]{:S(2)}) async-start(bf16[16,16,768]{2,1,0:T(8,128)(2,1)} %all_to_all.35), calls=%async_computation.6 | async-start | bytes 786432 | tf_op jit(solution)/shard_map/all_to_all | solution.py:286
  222.9 53.9 %copy-start.1 = (bf16[16,4,768]{2,1,0:T(4,128)(2,1)S(1)}, bf16[16,4,768]{2,1,0:T(4,128)(2,1)}, u32[]{:S(2)}) copy-start(bf16[16,4,768]{2,1,0:T(4,128)(2,1)} %param.4) | copy-start | bytes 294916
  223.3 52.7 %collective-permute-start.1 = (bf16[72,768]{1,0:T(8,128)(2,1)S(1)}, bf16[72,768]{1,0:T(8,128)(2,1)S(1)}, u32[]{:S(2)}, u32[]{:S(2)}) collective-permute-start(bf16[72,768]{1,0:T(8,128)(2,1)S(1)} %pad_maximum_fusion.1), channel_id=1, source_target_pairs={{0,0},{1,1},{2,2},{3,3},{64,4},{65,5},{66,6},{67,7},{128,8},{129,9... | collective-permute-start | bytes 331784 | tf_op jit(solution)/shard_map/ppermute | solution.py:282

commit v5 on v3

--- a/solution.py
+++ b/solution.py
@@ -183,7 +183,13 @@
     scale = lax.rsqrt(jnp.mean(as_float * as_float, axis=-1, keepdims=True) + epsilon)
     normalized = (as_float * scale).astype(jnp.bfloat16).reshape(clip_count * block, feature)
 
-    packed = with_scalars(normalized, scaled_weight)
+    lanes = 128
+    pieces = jnp.pad(jnp.stack(split(scaled_weight, 3)).reshape(-1), (0, lanes - 3 * per_device))
+    tail = jnp.broadcast_to(pieces, (clip_count, block, lanes))
+    spread = jnp.concatenate([normalized.reshape(clip_count, block, feature), tail], axis=2)
+    spread = lax.all_to_all(spread, "clip", 0, 0, tiled=True)
+    weight_rows = spread[:, 0, feature:]
+    spread = spread[:, :, :feature].reshape(clip_count * block, feature)
 
     grouped = pairs.reshape(owners, per_owner, 2)
     clips = jnp.arange(owners * clip_count, dtype=jnp.int32)
@@ -198,14 +204,39 @@
     chosen = mine[:, None, :] == slot_ids[None, :, None]
     chosen = chosen.reshape(owners * slots, clip_count).astype(jnp.bfloat16)
 
-    outgoing = dot(
-        spread_rows(chosen, block), normalized, ((1,), (0,)), jnp.bfloat16
-    ).reshape(owners, slots * block, feature)
+    depth = (slots + 1) * block
+    parts = 3
+    width = feature // parts
+    chunk = -(-parts * depth // 16) * 16
+    own = jnp.where(jnp.eye(owners, dtype=bool), slots, -1)
+    wanted = jnp.concatenate([mine, own], axis=1).astype(jnp.bfloat16)
+    out_row = jnp.arange(owners * chunk, dtype=jnp.int32)
+    in_row = jnp.arange(2 * clip_count * block, dtype=jnp.int32)
+    of_owner = out_row[:, None] // chunk == jnp.arange(owners, dtype=jnp.int32)[None, :]
+    of_source = jnp.arange(2 * clip_count, dtype=jnp.int32)[:, None] == in_row[None, :] // block
+    wanted = dot(of_owner.astype(jnp.bfloat16), wanted, ((1,), (0,)), jnp.bfloat16)
+    wanted = dot(wanted, of_source.astype(jnp.bfloat16), ((1,), (0,))).astype(jnp.int32)
+    out_part = (out_row % chunk // depth)[:, None]
+    out_depth = (out_row % chunk % depth)[:, None]
+    picked = (wanted == out_depth // block) & (out_depth % block == in_row[None, :] % block)
+    pick = [picked & (out_part == h) for h in range(parts)]
+    pick.append(of_owner & (out_part == parts) & (out_depth == 0))
+    pick = jnp.concatenate(pick, axis=1).astype(jnp.bfloat16)
+    sources = jnp.concatenate([normalized, spread], axis=0)
+    sources = [sources[:, h * width : (h + 1) * width] for h in range(parts)]
+    sources.append(jnp.pad(weight_rows, ((0, 0), (0, width - lanes))))
+    outgoing = dot(pick, jnp.concatenate(sources, axis=0), ((1,), (0,)), jnp.bfloat16)
+    outgoing = outgoing.reshape(owners, chunk, width)
     outgoing = lax.all_to_all(
         outgoing, "tm", 0, 0, axis_index_groups=long_range, tiled=True
     )
-    firsts, weight = without_scalars(lax.ppermute(packed, both, swap), per_device)
     partners = lax.all_to_all(outgoing, both, 0, 0, axis_index_groups=plane, tiled=True)
+    pieces = partners[0, parts * depth, : 3 * per_device].astype(jnp.float32)
+    pieces = pieces.reshape(3, per_device)
+    weight = (pieces[0] + pieces[1]) + pieces[2]
+    partners = jnp.concatenate(
+        [partners[:, h * depth : (h + 1) * depth] for h in range(parts)], axis=2
+    ).reshape(owners * depth, feature)
 
     owned = lax.dynamic_index_in_dim(grouped, owner, 0, keepdims=False)
     owned_rank = lax.dynamic_index_in_dim(rank, owner, 0, keepdims=False)
@@ -226,14 +257,21 @@
     partner_key = jnp.where(is_first, -1, row_key)
     first_spots = jnp.arange(clip_count * block, dtype=jnp.int32)
     partner_spots = jnp.arange(owners * slots * block, dtype=jnp.int32)
-    first_hot = (first_key[:, None] == first_spots[None, :]).astype(jnp.bfloat16)
-    partner_hot = (partner_key[:, None] == partner_spots[None, :]).astype(jnp.bfloat16)
     first_back = (first_spots[:, None] == first_key[None, :]).astype(jnp.bfloat16)
     partner_back = (partner_spots[:, None] == partner_key[None, :]).astype(jnp.bfloat16)
 
-    rows = dot(first_hot, firsts, ((1,), (0,)))
-    rows = rows + dot(partner_hot, partners.reshape(-1, feature), ((1,), (0,)))
-    rows = rows.astype(jnp.bfloat16).reshape(times, 2 * per_device * block, feature)
+    first_source = (first_slot - owner + owners * clip_count) % owners
+    entry_of = jnp.stack(
+        [
+            (first_source * depth + slots * block).reshape(times, per_device),
+            (source * depth + (partner_slot % slots) * block).reshape(times, per_device),
+        ],
+        axis=1,
+    ).reshape(-1)
+    entry = (jnp.repeat(entry_of, block) + row_index % block)[:, None]
+    entries = jnp.arange(owners * depth, dtype=jnp.int32)[None, :]
+    rows = dot((entry == entries).astype(jnp.bfloat16), partners, ((1,), (0,)), jnp.bfloat16)
+    rows = rows.reshape(times, 2 * per_device * block, feature)
     rows = lax.all_to_all(rows, both, 0, 0, axis_index_groups=home, tiled=True)
 
     my_ids = lax.dynamic_slice_in_dim(owned, place * per_device, per_device, 0)

time: 275 us -> 269 us (0.978)
  waiting for transfers between devices: 104 us -> 140 us
  blocking collectives: 41.7 us -> 13.9 us
  starting transfers between devices: 103 us -> 85.9 us
    all_to_all x1 -> x0, blocking collectives: 27.9 us -> none  [shards(): lax.all_to_all(grads, both, 0, 0, axis_index_groups=home, tiled=True)]
    all_to_all x0 -> x2, waiting for transfers between devices: none -> 24.6 us  [the longest x1 21.3 us: shards(): lax.all_to_all(grads, both, 0, 0, axis_index_groups=home, tiled=True)]
    all_to_all x0 -> x2, starting transfers between devices: none -> 23.2 us  [the longest x1 16.2 us: shards(): spread = lax.all_to_all(spread, 'clip', 0, 0, tiled=True)]
    all_to_all x1, starting transfers between devices: 19.2 us -> 5.74 us  [shards(): lax.all_to_all(outgoing, both, 0, 0, axis_index_groups=plane, tiled=True)]
    all_to_all x1, starting transfers between devices: 22.6 us -> 9.84 us  [shards(): lax.all_to_all(partner_sum, 'tm', 0, 0, axis_index_groups=long_range, til...]
    ppermute x1 -> x0, starting transfers between devices: 12.5 us -> none  [shards(): lax.ppermute(packed, both, swap)]
    all_to_all x1, waiting for transfers between devices: 38.5 us -> 48.9 us  [shards(): lax.all_to_all(outgoing, 'tm', 0, 0, axis_index_groups=long_range, tiled=...]
    all_to_all x1, starting transfers between devices: 28.5 us -> 19.4 us  [shards(): lax.all_to_all(outgoing, 'tm', 0, 0, axis_index_groups=long_range, tiled=...]
  transfers between devices with their start and end apart: 6 -> 7, of which waited for: 4 -> 6; matrix products, arithmetic and copies ran while one was open for 2% -> 2% of each run, Pallas kernels for 0% -> 0%
where the time goes in v5:
time: 269 us; the launch traced here: 264 us
  waiting for transfers between devices  140 us (52%)
  starting transfers between devices  85.9 us (32%)
  blocking collectives  13.9 us (5%)
  Pallas kernels  6.9 us (3%)
  other arithmetic  6.31 us (2%)
  matrix products  5.85 us (2%)
  local copies, waits for them, and re-layouts  3.58 us (1%)
    all_to_all x1, waiting for transfers between devices, shards(): lax.all_to_all(outgoing, 'tm', 0, 0, axis_index_groups=long_range, tiled=...  48.9 us
    ppermute x1, waiting for transfers between devices, shards(): first_sum = lax.ppermute(first_sum, both, back)  38.1 us
    all_to_all x1, waiting for transfers between devices, shards(): lax.all_to_all(grads, both, 0, 0, axis_index_groups=home, tiled=True)  21.3 us
    all_to_all x1, waiting for transfers between devices, shards(): rows = lax.all_to_all(rows, both, 0, 0, axis_index_groups=home, tiled=True)  20.7 us
    all_to_all x1, starting transfers between devices, shards(): lax.all_to_all(outgoing, 'tm', 0, 0, axis_index_groups=long_range, tiled=...  19.4 us
    all_to_all x1, starting transfers between devices, shards(): spread = lax.all_to_all(spread, 'clip', 0, 0, tiled=True)  16.2 us
    ppermute x1, starting transfers between devices, shards(): first_sum = lax.ppermute(first_sum, both, back)  14.5 us
    all_to_all x1, blocking collectives, shards(): lax.all_to_all(partner_sum, both, 0, 0, axis_index_groups=plane, tiled=True)  13.9 us
  transfers between devices with their start and end apart: 7, of which 6 were waited for; matrix products, arithmetic and copies ran while one was open for 2% of the time, Pallas kernels for 0%

profile of v5, /device:TPU:24, one launch (start us, length us, event | category | flops | bytes accessed | tf_op | source)
XLA Modules:
  0.0 263.6 jit_solution(9557695464664161144)
XLA Ops:
  0.6 1.0 fusion.39
  1.7 1.0 fusion.25
  2.7 0.7 fusion.103
  3.5 0.7 pad_maximum_fusion.1
  4.2 16.2 %all-to-all-start = ((bf16[16,4,896]{2,1,0:T(4,128)(2,1)}), bf16[16,4,896]{2,1,0:T(4,128)(2,1)S(1)}, u32[]{:S(2)}, u32[]{:S(2)}) async-start(bf16[16,4,896]{2,1,0:T(4,128)(2,1)} %pad_maximum_fusion.1), calls=%async_computation | async-start | bytes 229376 | tf_op jit(solution)/shard_map/all_to_all | solution.py:190
  20.5 0.7 copy.73
  22.0 0.6 broadcast_and_fusion.2
  22.7 3.4 %all-to-all-done = bf16[16,4,896]{2,1,0:T(4,128)(2,1)S(1)} async-done(((bf16[16,4,896]{2,1,0:T(4,128)(2,1)}), bf16[16,4,896]{2,1,0:T(4,128)(2,1)S(1)}, u32[]{:S(2)}, u32[]{:S(2)}) %all-to-all-start) | async-done | bytes 114720 | tf_op jit(solution)/shard_map/all_to_all | solution.py:190
  26.2 1.6 fusion.1
  27.8 19.4 %all-to-all-start.1 = ((bf16[16,64,256]{2,1,0:T(8,128)(2,1)}), bf16[16,64,256]{2,1,0:T(8,128)(2,1)}, u32[]{:S(2)}, u32[]{:S(2)}) async-start(bf16[16,64,256]{2,1,0:T(8,128)(2,1)} %bitcast.10), calls=%async_computation.1 | async-start | bytes 1048576 | tf_op jit(solution)/shard_map/all_to_all | solution.py:230
  48.2 48.9 %all-to-all-done.1 = bf16[16,64,256]{2,1,0:T(8,128)(2,1)} async-done(((bf16[16,64,256]{2,1,0:T(8,128)(2,1)}), bf16[16,64,256]{2,1,0:T(8,128)(2,1)}, u32[]{:S(2)}, u32[]{:S(2)}) %all-to-all-start.1) | async-done | bytes 524320 | tf_op jit(solution)/shard_map/all_to_all | solution.py:230
  97.1 5.7 %all-to-all-start.2 = ((bf16[16,64,256]{2,1,0:T(8,128)(2,1)}), bf16[16,64,256]{2,1,0:T(8,128)(2,1)S(1)}, u32[]{:S(2)}, u32[]{:S(2)}) async-start(bf16[16,64,256]{2,1,0:T(8,128)(2,1)} %all-to-all-done.1), calls=%async_computation.2 | async-start | bytes 1048576 | tf_op jit(solution)/shard_map/all_to_all | solution.py:233
  103.0 7.7 %all-to-all-done.2 = bf16[16,64,256]{2,1,0:T(8,128)(2,1)S(1)} async-done(((bf16[16,64,256]{2,1,0:T(8,128)(2,1)}), bf16[16,64,256]{2,1,0:T(8,128)(2,1)S(1)}, u32[]{:S(2)}, u32[]{:S(2)}) %all-to-all-start.2) | async-done | bytes 524320 | tf_op jit(solution)/shard_map/all_to_all | solution.py:233
  110.9 2.2 fusion.10
  113.1 13.2 %all-to-all-start.3 = ((bf16[64,16,768]{2,1,0:T(8,128)(2,1)}), bf16[64,16,768]{2,1,0:T(8,128)(2,1)S(1)}, u32[]{:S(2)}, u32[]{:S(2)}) async-start(bf16[64,16,768]{2,1,0:T(8,128)(2,1)} %fusion.10), calls=%async_computation.3 | async-start | bytes 3145728 | tf_op jit(solution)/shard_map/all_to_all | solution.py:275
  127.4 20.7 %all-to-all-done.3 = bf16[64,16,768]{2,1,0:T(8,128)(2,1)S(1)} async-done(((bf16[64,16,768]{2,1,0:T(8,128)(2,1)}), bf16[64,16,768]{2,1,0:T(8,128)(2,1)S(1)}, u32[]{:S(2)}, u32[]{:S(2)}) %all-to-all-start.3) | async-done | bytes 1572896 | tf_op jit(solution)/shard_map/all_to_all | solution.py:275
  148.1 6.9 %shard_map.59 = (bf16[1024,768]{1,0:T(8,128)(2,1)}, f32[2]{0:T(128)S(1)}) custom-call(s32[2,2]{1,0:T(2,128)S(1)} %and_select_fusion.5.length_ref, f32[2]{0:T(128)S(1)} %add_bitcast_fusion.1.weight_ref, bf16[1024,768]{1,0:T(8,128)(2,1)S(1)} %bitcast.59), custom_call_target="tpu_custom_call" | custom-call | tf_op jit(solution)/shard_map/pallas_call | solution.py:130
  155.0 6.9 %all-to-all-start.4 = ((bf16[64,16,768]{2,1,0:T(8,128)(2,1)}), bf16[64,16,768]{2,1,0:T(8,128)(2,1)S(1)}, u32[]{:S(2)}, u32[]{:S(2)}) async-start(bf16[64,16,768]{2,1,0:T(8,128)(2,1)} %bitcast.16), calls=%async_computation.4 | async-start | bytes 3145728 | tf_op jit(solution)/shard_map/all_to_all | solution.py:282
  162.5 21.3 %all-to-all-done.4 = bf16[64,16,768]{2,1,0:T(8,128)(2,1)S(1)} async-done(((bf16[64,16,768]{2,1,0:T(8,128)(2,1)}), bf16[64,16,768]{2,1,0:T(8,128)(2,1)S(1)}, u32[]{:S(2)}, u32[]{:S(2)}) %all-to-all-start.4) | async-done | bytes 1572896 | tf_op jit(solution)/shard_map/all_to_all | solution.py:282
  184.4 13.9 %all_to_all.35 = bf16[16,16,768]{2,1,0:T(8,128)(2,1)} all-to-all(bf16[16,16,768]{2,1,0:T(8,128)(2,1)S(1)} %bitcast.63), channel_id=1, replica_groups={{0,64,128,192,256,320,384,448,512,576,640,704,768,832,896,960},{1,65,12..., dimensions={0} | all-to-all | bytes 786432 | tf_op jit(solution)/shard_map/all_to_all | solution.py:289
  198.3 9.8 %all-to-all-start.6 = ((bf16[16,16,768]{2,1,0:T(8,128)(2,1)}), bf16[16,16,768]{2,1,0:T(8,128)(2,1)S(1)}, u32[]{:S(2)}, u32[]{:S(2)}) async-start(bf16[16,16,768]{2,1,0:T(8,128)(2,1)} %all_to_all.35), calls=%async_computation.6 | async-start | bytes 786432 | tf_op jit(solution)/shard_map/all_to_all | solution.py:291
  209.0 14.5 %collective-permute-start = (bf16[72,768]{1,0:T(8,128)(2,1)S(1)}, bf16[72,768]{1,0:T(8,128)(2,1)S(1)}, u32[]{:S(2)}, u32[]{:S(2)}) collective-permute-start(bf16[72,768]{1,0:T(8,128)(2,1)S(1)} %pad_maximum_fusion.2), channel_id=1, source_target_pairs={{0,0},{1,1},{2,2},{3,3},{64,4},{65,5},{66,6},{67,7},{128,8},{129,9... | collective-permute-start | bytes 331784 | tf_op jit(solution)/shard_map/ppermute | solution.py:287
  223.6 38.1 %collective-permute-done = bf16[72,768]{1,0:T(8,128)(2,1)S(1)} collective-permute-done((bf16[72,768]{1,0:T(8,128)(2,1)S(1)}, bf16[72,768]{1,0:T(8,128)(2,1)S(1)}, u32[]{:S(2)}, u32[]{:S(2)}) %collective-permute-start) | collective-permute-done | bytes 110624 | tf_op jit(solution)/shard_map/ppermute | solution.py:287
  262.7 0.9 fusion.38
  (84 shorter events, 6.4 us)
Async XLA Ops:
  0.6 125.9 %copy-start = (s32[256]{0:T(256)S(1)}, s32[256]{0:T(256)}, u32[]{:S(2)}) copy-start(s32[256]{0:T(256)} %param.5) | copy-start | bytes 3076
  4.2 21.9 %all-to-all-start = ((bf16[16,4,896]{2,1,0:T(4,128)(2,1)}), bf16[16,4,896]{2,1,0:T(4,128)(2,1)S(1)}, u32[]{:S(2)}, u32[]{:S(2)}) async-start(bf16[16,4,896]{2,1,0:T(4,128)(2,1)} %pad_maximum_fusion.1), calls=%async_computation | async-start | bytes 229376 | tf_op jit(solution)/shard_map/all_to_all | solution.py:190
  27.8 69.3 %all-to-all-start.1 = ((bf16[16,64,256]{2,1,0:T(8,128)(2,1)}), bf16[16,64,256]{2,1,0:T(8,128)(2,1)}, u32[]{:S(2)}, u32[]{:S(2)}) async-start(bf16[16,64,256]{2,1,0:T(8,128)(2,1)} %bitcast.10), calls=%async_computation.1 | async-start | bytes 1048576 | tf_op jit(solution)/shard_map/all_to_all | solution.py:230
  97.1 13.6 %all-to-all-start.2 = ((bf16[16,64,256]{2,1,0:T(8,128)(2,1)}), bf16[16,64,256]{2,1,0:T(8,128)(2,1)S(1)}, u32[]{:S(2)}, u32[]{:S(2)}) async-start(bf16[16,64,256]{2,1,0:T(8,128)(2,1)} %all-to-all-done.1), calls=%async_computation.2 | async-start | bytes 1048576 | tf_op jit(solution)/shard_map/all_to_all | solution.py:233
  113.1 35.0 %all-to-all-start.3 = ((bf16[64,16,768]{2,1,0:T(8,128)(2,1)}), bf16[64,16,768]{2,1,0:T(8,128)(2,1)S(1)}, u32[]{:S(2)}, u32[]{:S(2)}) async-start(bf16[64,16,768]{2,1,0:T(8,128)(2,1)} %fusion.10), calls=%async_computation.3 | async-start | bytes 3145728 | tf_op jit(solution)/shard_map/all_to_all | solution.py:275
  155.0 28.7 %all-to-all-start.4 = ((bf16[64,16,768]{2,1,0:T(8,128)(2,1)}), bf16[64,16,768]{2,1,0:T(8,128)(2,1)S(1)}, u32[]{:S(2)}, u32[]{:S(2)}) async-start(bf16[64,16,768]{2,1,0:T(8,128)(2,1)} %bitcast.16), calls=%async_computation.4 | async-start | bytes 3145728 | tf_op jit(solution)/shard_map/all_to_all | solution.py:282
  198.3 64.0 %all-to-all-start.6 = ((bf16[16,16,768]{2,1,0:T(8,128)(2,1)}), bf16[16,16,768]{2,1,0:T(8,128)(2,1)S(1)}, u32[]{:S(2)}, u32[]{:S(2)}) async-start(bf16[16,16,768]{2,1,0:T(8,128)(2,1)} %all_to_all.35), calls=%async_computation.6 | async-start | bytes 786432 | tf_op jit(solution)/shard_map/all_to_all | solution.py:291
  208.6 53.9 %copy-start.1 = (bf16[16,4,768]{2,1,0:T(4,128)(2,1)S(1)}, bf16[16,4,768]{2,1,0:T(4,128)(2,1)}, u32[]{:S(2)}) copy-start(bf16[16,4,768]{2,1,0:T(4,128)(2,1)} %param.4) | copy-start | bytes 294916
  209.0 52.7 %collective-permute-start = (bf16[72,768]{1,0:T(8,128)(2,1)S(1)}, bf16[72,768]{1,0:T(8,128)(2,1)S(1)}, u32[]{:S(2)}, u32[]{:S(2)}) collective-permute-start(bf16[72,768]{1,0:T(8,128)(2,1)S(1)} %pad_maximum_fusion.2), channel_id=1, source_target_pairs={{0,0},{1,1},{2,2},{3,3},{64,4},{65,5},{66,6},{67,7},{128,8},{129,9... | collective-permute-start | bytes 331784 | tf_op jit(solution)/shard_map/ppermute | solution.py:287

commit v6 on v5

--- a/solution.py
+++ b/solution.py
@@ -43,13 +43,13 @@
     factor = score_scale / math.sqrt(n_first.shape[1])
     scores = dot(n_first, n_partner, ((1,), (1,))) * factor
     forward_exp = jnp.where(column_time < len_partner, jnp.exp(scores), 0.0)
-    forward_prob = forward_exp / jnp.sum(forward_exp, axis=1, keepdims=True)
+    forward_prob = forward_exp * (1.0 / jnp.sum(forward_exp, axis=1, keepdims=True))
     prob = forward_prob.astype(jnp.bfloat16)
     high = scores.astype(jnp.bfloat16)
     low = (scores - high.astype(jnp.float32)).astype(jnp.bfloat16)
     backward_scores = dot(prob, high, ((1,), (1,))) + dot(prob, low, ((1,), (1,)))
     backward_exp = jnp.where(column_time < len_first, jnp.exp(backward_scores), 0.0)
-    back_prob = backward_exp / jnp.sum(backward_exp, axis=1, keepdims=True)
+    back_prob = backward_exp * (1.0 / jnp.sum(backward_exp, axis=1, keepdims=True))
     mean_time = jnp.sum(back_prob * column_time, axis=1, keepdims=True)
     offsets = column_time - mean_time
     squares = offsets * offsets
@@ -140,6 +140,11 @@
     )(lengths, weight, rows)
 
 
+def inverse_norm(rows):
+    as_float = rows.astype(jnp.float32)
+    return lax.rsqrt(jnp.mean(as_float * as_float, axis=-1, keepdims=True) + epsilon)
+
+
 def spread_rows(hot, block):
     rows = jnp.arange(hot.shape[0] * block, dtype=jnp.int32)
     columns = jnp.arange(hot.shape[1] * block, dtype=jnp.int32)
@@ -179,17 +184,18 @@
     back = [(there, here) for here, there in swap]
     both = ("clip", "tm")
 
-    as_float = embeddings.astype(jnp.float32)
-    scale = lax.rsqrt(jnp.mean(as_float * as_float, axis=-1, keepdims=True) + epsilon)
-    normalized = (as_float * scale).astype(jnp.bfloat16).reshape(clip_count * block, feature)
-
     lanes = 128
     pieces = jnp.pad(jnp.stack(split(scaled_weight, 3)).reshape(-1), (0, lanes - 3 * per_device))
     tail = jnp.broadcast_to(pieces, (clip_count, block, lanes))
-    spread = jnp.concatenate([normalized.reshape(clip_count, block, feature), tail], axis=2)
+    spread = jnp.concatenate([embeddings, tail], axis=2)
     spread = lax.all_to_all(spread, "clip", 0, 0, tiled=True)
     weight_rows = spread[:, 0, feature:]
     spread = spread[:, :, :feature].reshape(clip_count * block, feature)
+    spread = (spread.astype(jnp.float32) * inverse_norm(spread)).astype(jnp.bfloat16)
+    flat = embeddings.reshape(clip_count * block, feature)
+    scale = inverse_norm(flat)
+    unit = flat.astype(jnp.float32) * scale
+    normalized = unit.astype(jnp.bfloat16)
 
     grouped = pairs.reshape(owners, per_owner, 2)
     clips = jnp.arange(owners * clip_count, dtype=jnp.int32)
@@ -270,7 +276,8 @@
     ).reshape(-1)
     entry = (jnp.repeat(entry_of, block) + row_index % block)[:, None]
     entries = jnp.arange(owners * depth, dtype=jnp.int32)[None, :]
-    rows = dot((entry == entries).astype(jnp.bfloat16), partners, ((1,), (0,)), jnp.bfloat16)
+    entry_hot = lax.optimization_barrier((entry == entries).astype(jnp.bfloat16))
+    rows = dot(entry_hot, partners, ((1,), (0,)), jnp.bfloat16)
     rows = rows.reshape(times, 2 * per_device * block, feature)
     rows = lax.all_to_all(rows, both, 0, 0, axis_index_groups=home, tiled=True)
 
@@ -292,9 +299,9 @@
         partner_sum, "tm", 0, 0, axis_index_groups=long_range, tiled=True
     )
     total = dot(spread_rows(chosen.T, block), partner_sum.reshape(-1, feature), ((1,), (0,)))
-    total = (total + first_sum.astype(jnp.float32)).reshape(clip_count, block, feature)
-    unit = as_float * scale
+    total = total + first_sum.astype(jnp.float32)
     gradient = scale * (total - unit * jnp.mean(total * unit, axis=-1, keepdims=True))
+    gradient = gradient.reshape(clip_count, block, feature)
     return (losses, gradient.astype(jnp.bfloat16))
 
 

time: 269 us -> 268 us (level)
  transfers between devices with their start and end apart: 7 -> 7, of which waited for: 6 -> 6; matrix products, arithmetic and copies ran while one was open for 2% -> 3% of each run, Pallas kernels for 0% -> 0%
where the time goes in v6:
time: 268 us; the launch traced here: 263 us
  waiting for transfers between devices  138 us (51%)
  starting transfers between devices  85.9 us (32%)
  blocking collectives  13.9 us (5%)
  Pallas kernels  6.88 us (3%)
  matrix products  5.88 us (2%)
  other arithmetic  5.8 us (2%)
  local copies, waits for them, and re-layouts  5.49 us (2%)
    all_to_all x1, waiting for transfers between devices, shards(): lax.all_to_all(outgoing, 'tm', 0, 0, axis_index_groups=long_range, tiled=...  49.1 us
    ppermute x1, waiting for transfers between devices, shards(): first_sum = lax.ppermute(first_sum, both, back)  38.2 us
    all_to_all x1, waiting for transfers between devices, shards(): lax.all_to_all(grads, both, 0, 0, axis_index_groups=home, tiled=True)  21.1 us
    all_to_all x1, waiting for transfers between devices, shards(): rows = lax.all_to_all(rows, both, 0, 0, axis_index_groups=home, tiled=True)  20.7 us
    all_to_all x1, starting transfers between devices, shards(): lax.all_to_all(outgoing, 'tm', 0, 0, axis_index_groups=long_range, tiled=...  19.4 us
    all_to_all x1, starting transfers between devices, shards(): spread = lax.all_to_all(spread, 'clip', 0, 0, tiled=True)  16.2 us
    ppermute x1, starting transfers between devices, shards(): first_sum = lax.ppermute(first_sum, both, back)  14.3 us
    all_to_all x1, blocking collectives, shards(): lax.all_to_all(partner_sum, both, 0, 0, axis_index_groups=plane, tiled=True)  13.9 us
  transfers between devices with their start and end apart: 7, of which 6 were waited for; matrix products, arithmetic and copies ran while one was open for 3% of the time, Pallas kernels for 0%

profile of v6, /device:TPU:24, one launch (start us, length us, event | category | flops | bytes accessed | tf_op | source)
XLA Modules:
  0.0 262.6 jit_solution(188122501737713564)
XLA Ops:
  0.6 0.7 fusion.98
  1.4 1.6 pad_maximum_fusion.2
  3.0 16.2 %all-to-all-start = ((bf16[16,4,896]{2,1,0:T(4,128)(2,1)}), bf16[16,4,896]{2,1,0:T(4,128)(2,1)S(1)}, u32[]{:S(2)}, u32[]{:S(2)}) async-start(bf16[16,4,896]{2,1,0:T(4,128)(2,1)} %pad_maximum_fusion.2), calls=%async_computation | async-start | bytes 229376 | tf_op jit(solution)/shard_map/all_to_all | solution.py:191
  19.3 1.0 multiply_reduce_fusion.2
  20.4 0.9 reshape.766
  21.4 0.7 copy.69
  23.0 0.6 broadcast_and_fusion.2
  23.6 1.3 all-to-all-done
  25.4 1.6 fusion.1
  27.0 19.4 %all-to-all-start.1 = ((bf16[16,64,256]{2,1,0:T(8,128)(2,1)}), bf16[16,64,256]{2,1,0:T(8,128)(2,1)}, u32[]{:S(2)}, u32[]{:S(2)}) async-start(bf16[16,64,256]{2,1,0:T(8,128)(2,1)} %bitcast.10), calls=%async_computation.1 | async-start | bytes 1048576 | tf_op jit(solution)/shard_map/all_to_all | solution.py:236
  47.2 49.1 %all-to-all-done.1 = bf16[16,64,256]{2,1,0:T(8,128)(2,1)} async-done(((bf16[16,64,256]{2,1,0:T(8,128)(2,1)}), bf16[16,64,256]{2,1,0:T(8,128)(2,1)}, u32[]{:S(2)}, u32[]{:S(2)}) %all-to-all-start.1) | async-done | bytes 524320 | tf_op jit(solution)/shard_map/all_to_all | solution.py:236
  96.3 6.5 %all-to-all-start.2 = ((bf16[16,64,256]{2,1,0:T(8,128)(2,1)}), bf16[16,64,256]{2,1,0:T(8,128)(2,1)S(1)}, u32[]{:S(2)}, u32[]{:S(2)}) async-start(bf16[16,64,256]{2,1,0:T(8,128)(2,1)} %all-to-all-done.1), calls=%async_computation.2 | async-start | bytes 1048576 | tf_op jit(solution)/shard_map/all_to_all | solution.py:239
  103.5 7.2 %all-to-all-done.2 = bf16[16,64,256]{2,1,0:T(8,128)(2,1)S(1)} async-done(((bf16[16,64,256]{2,1,0:T(8,128)(2,1)}), bf16[16,64,256]{2,1,0:T(8,128)(2,1)S(1)}, u32[]{:S(2)}, u32[]{:S(2)}) %all-to-all-start.2) | async-done | bytes 524320 | tf_op jit(solution)/shard_map/all_to_all | solution.py:239
  110.9 2.1 fusion.118
  113.0 13.6 %all-to-all-start.3 = ((bf16[64,16,768]{2,1,0:T(8,128)(2,1)}), bf16[64,16,768]{2,1,0:T(8,128)(2,1)S(1)}, u32[]{:S(2)}, u32[]{:S(2)}) async-start(bf16[64,16,768]{2,1,0:T(8,128)(2,1)} %fusion.118), calls=%async_computation.3 | async-start | bytes 3145728 | tf_op jit(solution)/shard_map/all_to_all | solution.py:282
  127.7 20.7 %all-to-all-done.3 = bf16[64,16,768]{2,1,0:T(8,128)(2,1)S(1)} async-done(((bf16[64,16,768]{2,1,0:T(8,128)(2,1)}), bf16[64,16,768]{2,1,0:T(8,128)(2,1)S(1)}, u32[]{:S(2)}, u32[]{:S(2)}) %all-to-all-start.3) | async-done | bytes 1572896 | tf_op jit(solution)/shard_map/all_to_all | solution.py:282
  148.4 6.9 %shard_map.59 = (bf16[1024,768]{1,0:T(8,128)(2,1)}, f32[2]{0:T(128)S(1)}) custom-call(s32[2,2]{1,0:T(2,128)S(1)} %and_select_fusion.3.length_ref, f32[2]{0:T(128)S(1)} %add_bitcast_fusion.1.weight_ref, bf16[1024,768]{1,0:T(8,128)(2,1)S(1)} %bitcast.56), custom_call_target="tpu_custom_call" | custom-call | tf_op jit(solution)/shard_map/pallas_call | solution.py:130
  155.3 6.9 %all-to-all-start.4 = ((bf16[64,16,768]{2,1,0:T(8,128)(2,1)}), bf16[64,16,768]{2,1,0:T(8,128)(2,1)S(1)}, u32[]{:S(2)}, u32[]{:S(2)}) async-start(bf16[64,16,768]{2,1,0:T(8,128)(2,1)} %bitcast.14), calls=%async_computation.4 | async-start | bytes 3145728 | tf_op jit(solution)/shard_map/all_to_all | solution.py:289
  162.9 21.1 %all-to-all-done.4 = bf16[64,16,768]{2,1,0:T(8,128)(2,1)S(1)} async-done(((bf16[64,16,768]{2,1,0:T(8,128)(2,1)}), bf16[64,16,768]{2,1,0:T(8,128)(2,1)S(1)}, u32[]{:S(2)}, u32[]{:S(2)}) %all-to-all-start.4) | async-done | bytes 1572896 | tf_op jit(solution)/shard_map/all_to_all | solution.py:289
  184.6 13.9 %all_to_all.35 = bf16[16,16,768]{2,1,0:T(8,128)(2,1)} all-to-all(bf16[16,16,768]{2,1,0:T(8,128)(2,1)S(1)} %bitcast.61), channel_id=1, replica_groups={{0,64,128,192,256,320,384,448,512,576,640,704,768,832,896,960},{1,65,12..., dimensions={0} | all-to-all | bytes 786432 | tf_op jit(solution)/shard_map/all_to_all | solution.py:296
  198.5 8.8 %all-to-all-start.6 = ((bf16[16,16,768]{2,1,0:T(8,128)(2,1)}), bf16[16,16,768]{2,1,0:T(8,128)(2,1)S(1)}, u32[]{:S(2)}, u32[]{:S(2)}) async-start(bf16[16,16,768]{2,1,0:T(8,128)(2,1)} %all_to_all.35), calls=%async_computation.6 | async-start | bytes 786432 | tf_op jit(solution)/shard_map/all_to_all | solution.py:298
  208.2 14.3 %collective-permute-start = (bf16[72,768]{1,0:T(8,128)(2,1)S(1)}, bf16[72,768]{1,0:T(8,128)(2,1)S(1)}, u32[]{:S(2)}, u32[]{:S(2)}) collective-permute-start(bf16[72,768]{1,0:T(8,128)(2,1)S(1)} %pad_maximum_fusion.3), channel_id=1, source_target_pairs={{0,0},{1,1},{2,2},{3,3},{64,4},{65,5},{66,6},{67,7},{128,8},{129,9... | collective-permute-start | bytes 331784 | tf_op jit(solution)/shard_map/ppermute | solution.py:294
  222.7 38.2 %collective-permute-done = bf16[72,768]{1,0:T(8,128)(2,1)S(1)} collective-permute-done((bf16[72,768]{1,0:T(8,128)(2,1)S(1)}, bf16[72,768]{1,0:T(8,128)(2,1)S(1)}, u32[]{:S(2)}, u32[]{:S(2)}) %collective-permute-start) | collective-permute-done | bytes 110624 | tf_op jit(solution)/shard_map/ppermute | solution.py:294
  261.9 0.7 convert_element_type.115
  (85 shorter events, 7.2 us)
Async XLA Ops:
  0.6 126.2 %copy-start = (s32[256]{0:T(256)S(1)}, s32[256]{0:T(256)}, u32[]{:S(2)}) copy-start(s32[256]{0:T(256)} %param.5) | copy-start | bytes 3076
  3.0 21.9 %all-to-all-start = ((bf16[16,4,896]{2,1,0:T(4,128)(2,1)}), bf16[16,4,896]{2,1,0:T(4,128)(2,1)S(1)}, u32[]{:S(2)}, u32[]{:S(2)}) async-start(bf16[16,4,896]{2,1,0:T(4,128)(2,1)} %pad_maximum_fusion.2), calls=%async_computation | async-start | bytes 229376 | tf_op jit(solution)/shard_map/all_to_all | solution.py:191
  27.0 69.3 %all-to-all-start.1 = ((bf16[16,64,256]{2,1,0:T(8,128)(2,1)}), bf16[16,64,256]{2,1,0:T(8,128)(2,1)}, u32[]{:S(2)}, u32[]{:S(2)}) async-start(bf16[16,64,256]{2,1,0:T(8,128)(2,1)} %bitcast.10), calls=%async_computation.1 | async-start | bytes 1048576 | tf_op jit(solution)/shard_map/all_to_all | solution.py:236
  96.3 14.4 %all-to-all-start.2 = ((bf16[16,64,256]{2,1,0:T(8,128)(2,1)}), bf16[16,64,256]{2,1,0:T(8,128)(2,1)S(1)}, u32[]{:S(2)}, u32[]{:S(2)}) async-start(bf16[16,64,256]{2,1,0:T(8,128)(2,1)} %all-to-all-done.1), calls=%async_computation.2 | async-start | bytes 1048576 | tf_op jit(solution)/shard_map/all_to_all | solution.py:239
  113.0 35.4 %all-to-all-start.3 = ((bf16[64,16,768]{2,1,0:T(8,128)(2,1)}), bf16[64,16,768]{2,1,0:T(8,128)(2,1)S(1)}, u32[]{:S(2)}, u32[]{:S(2)}) async-start(bf16[64,16,768]{2,1,0:T(8,128)(2,1)} %fusion.118), calls=%async_computation.3 | async-start | bytes 3145728 | tf_op jit(solution)/shard_map/all_to_all | solution.py:282
  155.3 28.7 %all-to-all-start.4 = ((bf16[64,16,768]{2,1,0:T(8,128)(2,1)}), bf16[64,16,768]{2,1,0:T(8,128)(2,1)S(1)}, u32[]{:S(2)}, u32[]{:S(2)}) async-start(bf16[64,16,768]{2,1,0:T(8,128)(2,1)} %bitcast.14), calls=%async_computation.4 | async-start | bytes 3145728 | tf_op jit(solution)/shard_map/all_to_all | solution.py:289
  198.5 62.9 %all-to-all-start.6 = ((bf16[16,16,768]{2,1,0:T(8,128)(2,1)}), bf16[16,16,768]{2,1,0:T(8,128)(2,1)S(1)}, u32[]{:S(2)}, u32[]{:S(2)}) async-start(bf16[16,16,768]{2,1,0:T(8,128)(2,1)} %all_to_all.35), calls=%async_computation.6 | async-start | bytes 786432 | tf_op jit(solution)/shard_map/all_to_all | solution.py:298
  208.2 52.7 %collective-permute-start = (bf16[72,768]{1,0:T(8,128)(2,1)S(1)}, bf16[72,768]{1,0:T(8,128)(2,1)S(1)}, u32[]{:S(2)}, u32[]{:S(2)}) collective-permute-start(bf16[72,768]{1,0:T(8,128)(2,1)S(1)} %pad_maximum_fusion.3), channel_id=1, source_target_pairs={{0,0},{1,1},{2,2},{3,3},{64,4},{65,5},{66,6},{67,7},{128,8},{129,9... | collective-permute-start | bytes 331784 | tf_op jit(solution)/shard_map/ppermute | solution.py:294

commit v7 on v6

--- a/solution.py
+++ b/solution.py
@@ -80,17 +80,20 @@
     chunk = 2 * count * block
     sources = total // chunk
     frames = sources * block
+    pitch = chunk + 1
     lanes = wide.shape[2]
     strips = wide.shape[0]
     for c in range(strips):
-        wide[c] = rows_ref[:, c * lanes : (c + 1) * lanes].astype(jnp.float32)
+        strip = rows_ref[:, c * lanes : (c + 1) * lanes].astype(jnp.float32)
+        for d in range(sources):
+            wide[c, d * pitch : d * pitch + chunk] = strip[d * chunk : (d + 1) * chunk]
     row = lax.broadcasted_iota(jnp.int32, (frames, 1), 0)
     row_time = ((row % sources) * block + row // sources).astype(jnp.float32)
     column = lax.broadcasted_iota(jnp.int32, (1, frames), 1)
     column_time = ((column % sources) * block + column // sources).astype(jnp.float32)
 
     def place(kind, pair, frame):
-        return pl.ds((kind * count + pair) * block + frame, sources, stride=chunk)
+        return pl.ds((kind * count + pair) * block + frame, sources, stride=pitch)
 
     for pair in range(count):
         clips = [
@@ -121,10 +124,15 @@
                 for c in range(strips):
                     wide[c, place(kind, pair, f), :] = part[:, c * lanes : (c + 1) * lanes]
     for c in range(strips):
-        out_ref[:, c * lanes : (c + 1) * lanes] = wide[c].astype(jnp.bfloat16)
+        for d in range(sources):
+            part = wide[c, d * pitch : d * pitch + chunk]
+            out_ref[d * chunk : (d + 1) * chunk, c * lanes : (c + 1) * lanes] = part.astype(
+                jnp.bfloat16
+            )
 
 
 def pair_call(rows, lengths, weight, block):
+    padded = rows.shape[0] + rows.shape[0] // (2 * weight.shape[0] * block)
     smem = pl.BlockSpec(memory_space=pltpu.SMEM)
     vmem = pl.BlockSpec(memory_space=pltpu.VMEM)
     return pl.pallas_call(
@@ -135,7 +143,7 @@
         ),
         in_specs=[smem, smem, vmem],
         out_specs=(vmem, smem),
-        scratch_shapes=[pltpu.VMEM((rows.shape[1] // 128, rows.shape[0], 128), jnp.float32)],
+        scratch_shapes=[pltpu.VMEM((rows.shape[1] // 128, padded, 128), jnp.float32)],
         compiler_params=pltpu.CompilerParams(vmem_limit_bytes=40 * 1024 * 1024),
     )(lengths, weight, rows)
 

time: 268 us -> 266 us (level)
  no operation moved by 1% of the time
where the time goes in v7:
time: 266 us; the launch traced here: 261 us
  waiting for transfers between devices  138 us (52%)
  starting transfers between devices  85.9 us (32%)
  blocking collectives  13.9 us (5%)
  matrix products  5.88 us (2%)
  other arithmetic  5.8 us (2%)
  local copies, waits for them, and re-layouts  5.49 us (2%)
  Pallas kernels  5.28 us (2%)
    all_to_all x1, waiting for transfers between devices, shards(): lax.all_to_all(outgoing, 'tm', 0, 0, axis_index_groups=long_range, tiled=...  49.1 us
    ppermute x1, waiting for transfers between devices, shards(): first_sum = lax.ppermute(first_sum, both, back)  38.2 us
    all_to_all x1, waiting for transfers between devices, shards(): lax.all_to_all(grads, both, 0, 0, axis_index_groups=home, tiled=True)  21.1 us
    all_to_all x1, waiting for transfers between devices, shards(): rows = lax.all_to_all(rows, both, 0, 0, axis_index_groups=home, tiled=True)  20.7 us
    all_to_all x1, starting transfers between devices, shards(): lax.all_to_all(outgoing, 'tm', 0, 0, axis_index_groups=long_range, tiled=...  19.4 us
    all_to_all x1, starting transfers between devices, shards(): spread = lax.all_to_all(spread, 'clip', 0, 0, tiled=True)  16.2 us
    ppermute x1, starting transfers between devices, shards(): first_sum = lax.ppermute(first_sum, both, back)  14.3 us
    all_to_all x1, blocking collectives, shards(): lax.all_to_all(partner_sum, both, 0, 0, axis_index_groups=plane, tiled=True)  13.9 us
  transfers between devices with their start and end apart: 7, of which 6 were waited for; matrix products, arithmetic and copies ran while one was open for 3% of the time, Pallas kernels for 0%

profile of v7, /device:TPU:24, one launch (start us, length us, event | category | flops | bytes accessed | tf_op | source)
XLA Modules:
  0.0 261.0 jit_solution(12736351652157963541)
XLA Ops:
  0.6 0.7 fusion.98
  1.4 1.6 pad_maximum_fusion.2
  3.0 16.2 %all-to-all-start = ((bf16[16,4,896]{2,1,0:T(4,128)(2,1)}), bf16[16,4,896]{2,1,0:T(4,128)(2,1)S(1)}, u32[]{:S(2)}, u32[]{:S(2)}) async-start(bf16[16,4,896]{2,1,0:T(4,128)(2,1)} %pad_maximum_fusion.2), calls=%async_computation | async-start | bytes 229376 | tf_op jit(solution)/shard_map/all_to_all | solution.py:199
  19.3 1.0 multiply_reduce_fusion.2
  20.4 0.9 reshape.766
  21.4 0.7 copy.69
  23.0 0.6 broadcast_and_fusion.2
  23.6 1.3 all-to-all-done
  25.4 1.6 fusion.1
  27.0 19.4 %all-to-all-start.1 = ((bf16[16,64,256]{2,1,0:T(8,128)(2,1)}), bf16[16,64,256]{2,1,0:T(8,128)(2,1)}, u32[]{:S(2)}, u32[]{:S(2)}) async-start(bf16[16,64,256]{2,1,0:T(8,128)(2,1)} %bitcast.10), calls=%async_computation.1 | async-start | bytes 1048576 | tf_op jit(solution)/shard_map/all_to_all | solution.py:244
  47.2 49.1 %all-to-all-done.1 = bf16[16,64,256]{2,1,0:T(8,128)(2,1)} async-done(((bf16[16,64,256]{2,1,0:T(8,128)(2,1)}), bf16[16,64,256]{2,1,0:T(8,128)(2,1)}, u32[]{:S(2)}, u32[]{:S(2)}) %all-to-all-start.1) | async-done | bytes 524320 | tf_op jit(solution)/shard_map/all_to_all | solution.py:244
  96.3 6.5 %all-to-all-start.2 = ((bf16[16,64,256]{2,1,0:T(8,128)(2,1)}), bf16[16,64,256]{2,1,0:T(8,128)(2,1)S(1)}, u32[]{:S(2)}, u32[]{:S(2)}) async-start(bf16[16,64,256]{2,1,0:T(8,128)(2,1)} %all-to-all-done.1), calls=%async_computation.2 | async-start | bytes 1048576 | tf_op jit(solution)/shard_map/all_to_all | solution.py:247
  103.5 7.2 %all-to-all-done.2 = bf16[16,64,256]{2,1,0:T(8,128)(2,1)S(1)} async-done(((bf16[16,64,256]{2,1,0:T(8,128)(2,1)}), bf16[16,64,256]{2,1,0:T(8,128)(2,1)S(1)}, u32[]{:S(2)}, u32[]{:S(2)}) %all-to-all-start.2) | async-done | bytes 524320 | tf_op jit(solution)/shard_map/all_to_all | solution.py:247
  110.9 2.1 fusion.118
  113.0 13.6 %all-to-all-start.3 = ((bf16[64,16,768]{2,1,0:T(8,128)(2,1)}), bf16[64,16,768]{2,1,0:T(8,128)(2,1)S(1)}, u32[]{:S(2)}, u32[]{:S(2)}) async-start(bf16[64,16,768]{2,1,0:T(8,128)(2,1)} %fusion.118), calls=%async_computation.3 | async-start | bytes 3145728 | tf_op jit(solution)/shard_map/all_to_all | solution.py:290
  127.7 20.7 %all-to-all-done.3 = bf16[64,16,768]{2,1,0:T(8,128)(2,1)S(1)} async-done(((bf16[64,16,768]{2,1,0:T(8,128)(2,1)}), bf16[64,16,768]{2,1,0:T(8,128)(2,1)S(1)}, u32[]{:S(2)}, u32[]{:S(2)}) %all-to-all-start.3) | async-done | bytes 1572896 | tf_op jit(solution)/shard_map/all_to_all | solution.py:290
  148.4 5.3 %shard_map.59 = (bf16[1024,768]{1,0:T(8,128)(2,1)}, f32[2]{0:T(128)S(1)}) custom-call(s32[2,2]{1,0:T(2,128)S(1)} %and_select_fusion.3.length_ref, f32[2]{0:T(128)S(1)} %add_bitcast_fusion.1.weight_ref, bf16[1024,768]{1,0:T(8,128)(2,1)S(1)} %bitcast.56), custom_call_target="tpu_custom_call" | custom-call | tf_op jit(solution)/shard_map/pallas_call | solution.py:138
  153.7 6.9 %all-to-all-start.4 = ((bf16[64,16,768]{2,1,0:T(8,128)(2,1)}), bf16[64,16,768]{2,1,0:T(8,128)(2,1)S(1)}, u32[]{:S(2)}, u32[]{:S(2)}) async-start(bf16[64,16,768]{2,1,0:T(8,128)(2,1)} %bitcast.14), calls=%async_computation.4 | async-start | bytes 3145728 | tf_op jit(solution)/shard_map/all_to_all | solution.py:297
  161.3 21.1 %all-to-all-done.4 = bf16[64,16,768]{2,1,0:T(8,128)(2,1)S(1)} async-done(((bf16[64,16,768]{2,1,0:T(8,128)(2,1)}), bf16[64,16,768]{2,1,0:T(8,128)(2,1)S(1)}, u32[]{:S(2)}, u32[]{:S(2)}) %all-to-all-start.4) | async-done | bytes 1572896 | tf_op jit(solution)/shard_map/all_to_all | solution.py:297
  183.0 13.9 %all_to_all.35 = bf16[16,16,768]{2,1,0:T(8,128)(2,1)} all-to-all(bf16[16,16,768]{2,1,0:T(8,128)(2,1)S(1)} %bitcast.61), channel_id=1, replica_groups={{0,64,128,192,256,320,384,448,512,576,640,704,768,832,896,960},{1,65,12..., dimensions={0} | all-to-all | bytes 786432 | tf_op jit(solution)/shard_map/all_to_all | solution.py:304
  196.9 8.8 %all-to-all-start.6 = ((bf16[16,16,768]{2,1,0:T(8,128)(2,1)}), bf16[16,16,768]{2,1,0:T(8,128)(2,1)S(1)}, u32[]{:S(2)}, u32[]{:S(2)}) async-start(bf16[16,16,768]{2,1,0:T(8,128)(2,1)} %all_to_all.35), calls=%async_computation.6 | async-start | bytes 786432 | tf_op jit(solution)/shard_map/all_to_all | solution.py:306
  206.6 14.3 %collective-permute-start = (bf16[72,768]{1,0:T(8,128)(2,1)S(1)}, bf16[72,768]{1,0:T(8,128)(2,1)S(1)}, u32[]{:S(2)}, u32[]{:S(2)}) collective-permute-start(bf16[72,768]{1,0:T(8,128)(2,1)S(1)} %pad_maximum_fusion.3), channel_id=1, source_target_pairs={{0,0},{1,1},{2,2},{3,3},{64,4},{65,5},{66,6},{67,7},{128,8},{129,9... | collective-permute-start | bytes 331784 | tf_op jit(solution)/shard_map/ppermute | solution.py:302
  221.1 38.2 %collective-permute-done = bf16[72,768]{1,0:T(8,128)(2,1)S(1)} collective-permute-done((bf16[72,768]{1,0:T(8,128)(2,1)S(1)}, bf16[72,768]{1,0:T(8,128)(2,1)S(1)}, u32[]{:S(2)}, u32[]{:S(2)}) %collective-permute-start) | collective-permute-done | bytes 110624 | tf_op jit(solution)/shard_map/ppermute | solution.py:302
  260.3 0.7 convert_element_type.115
  (85 shorter events, 7.2 us)
Async XLA Ops:
  0.6 126.2 %copy-start = (s32[256]{0:T(256)S(1)}, s32[256]{0:T(256)}, u32[]{:S(2)}) copy-start(s32[256]{0:T(256)} %param.5) | copy-start | bytes 3076
  3.0 21.9 %all-to-all-start = ((bf16[16,4,896]{2,1,0:T(4,128)(2,1)}), bf16[16,4,896]{2,1,0:T(4,128)(2,1)S(1)}, u32[]{:S(2)}, u32[]{:S(2)}) async-start(bf16[16,4,896]{2,1,0:T(4,128)(2,1)} %pad_maximum_fusion.2), calls=%async_computation | async-start | bytes 229376 | tf_op jit(solution)/shard_map/all_to_all | solution.py:199
  27.0 69.3 %all-to-all-start.1 = ((bf16[16,64,256]{2,1,0:T(8,128)(2,1)}), bf16[16,64,256]{2,1,0:T(8,128)(2,1)}, u32[]{:S(2)}, u32[]{:S(2)}) async-start(bf16[16,64,256]{2,1,0:T(8,128)(2,1)} %bitcast.10), calls=%async_computation.1 | async-start | bytes 1048576 | tf_op jit(solution)/shard_map/all_to_all | solution.py:244
  96.3 14.4 %all-to-all-start.2 = ((bf16[16,64,256]{2,1,0:T(8,128)(2,1)}), bf16[16,64,256]{2,1,0:T(8,128)(2,1)S(1)}, u32[]{:S(2)}, u32[]{:S(2)}) async-start(bf16[16,64,256]{2,1,0:T(8,128)(2,1)} %all-to-all-done.1), calls=%async_computation.2 | async-start | bytes 1048576 | tf_op jit(solution)/shard_map/all_to_all | solution.py:247
  113.0 35.4 %all-to-all-start.3 = ((bf16[64,16,768]{2,1,0:T(8,128)(2,1)}), bf16[64,16,768]{2,1,0:T(8,128)(2,1)S(1)}, u32[]{:S(2)}, u32[]{:S(2)}) async-start(bf16[64,16,768]{2,1,0:T(8,128)(2,1)} %fusion.118), calls=%async_computation.3 | async-start | bytes 3145728 | tf_op jit(solution)/shard_map/all_to_all | solution.py:290
  153.7 28.7 %all-to-all-start.4 = ((bf16[64,16,768]{2,1,0:T(8,128)(2,1)}), bf16[64,16,768]{2,1,0:T(8,128)(2,1)S(1)}, u32[]{:S(2)}, u32[]{:S(2)}) async-start(bf16[64,16,768]{2,1,0:T(8,128)(2,1)} %bitcast.14), calls=%async_computation.4 | async-start | bytes 3145728 | tf_op jit(solution)/shard_map/all_to_all | solution.py:297
  196.9 62.9 %all-to-all-start.6 = ((bf16[16,16,768]{2,1,0:T(8,128)(2,1)}), bf16[16,16,768]{2,1,0:T(8,128)(2,1)S(1)}, u32[]{:S(2)}, u32[]{:S(2)}) async-start(bf16[16,16,768]{2,1,0:T(8,128)(2,1)} %all_to_all.35), calls=%async_computation.6 | async-start | bytes 786432 | tf_op jit(solution)/shard_map/all_to_all | solution.py:306
  206.6 52.7 %collective-permute-start = (bf16[72,768]{1,0:T(8,128)(2,1)S(1)}, bf16[72,768]{1,0:T(8,128)(2,1)S(1)}, u32[]{:S(2)}, u32[]{:S(2)}) collective-permute-start(bf16[72,768]{1,0:T(8,128)(2,1)S(1)} %pad_maximum_fusion.3), channel_id=1, source_target_pairs={{0,0},{1,1},{2,2},{3,3},{64,4},{65,5},{66,6},{67,7},{128,8},{129,9... | collective-permute-start | bytes 331784 | tf_op jit(solution)/shard_map/ppermute | solution.py:302
